TPU v7x, 128 devices: a whole 4x4x4 slice. The times are simulated.
128 devices in a mesh: seq: 32 (over z, y, core), head: 4 (over x).
Axes of the slice: x: 4, y: 4, z: 4, core: 2. Of those that a mesh axis runs over, the one named last changes fastest.
Arguments:
- tokens_x: float32 [32768, 4096], P('seq', 'head'), may hold values from -0.06 to 0.06
- keys: float32 [32768, 32, 128], P('seq', 'head'), may hold values from -0.09375 to 0.09375
- values: float32 [32768, 32, 128], P('seq', 'head'), may hold values from -0.5 to 0.5
- grad_out: float32 [32768, 32, 128], P('seq', 'head'), may hold values from -6 to 6
- level_table: float32 [32, 16, 17], P('head'), may hold values from 0.05 to 1
- level_bins: int32 [32768, 32], P('seq', 'head'), may hold values from 0 to 15
Outputs:
- grad_query: float32 [32768, 32, 128], P('seq', 'head')
- grad_wq: float32 [4096, 4096], P('seq', 'head')
All inputs are finite; a program needn't handle non-finite values.
Results may differ from a plain program's by a relative error of at most 0.00011.
Values sent between devices are 32-bit elements; how exact they have to be, the bound alone decides.
A program may use at most 192 MiB of HBM per device.

v0:
```python
import jax
import jax.numpy as jnp
import numpy as np
from jax import lax
from jax.sharding import PartitionSpec as P

HIGH = lax.Precision.HIGHEST


def level_map(count):
    later = np.arange(count)[:, None]
    earlier = np.arange(count)[None, :]
    differ = later ^ earlier
    result = np.zeros((count, count), np.int64)
    for place in range(24):
        result = result + (differ >> place > 0)
    return np.where(earlier <= later, result, -1).astype(np.int32)


def read_state(state, grad_out):
    return jnp.einsum("hde,the->thd", state, grad_out, precision=HIGH)


def body(tokens_x, keys, values, grad_out, level_table, level_bins):
    width, local_heads, head_size = keys.shape
    bins_count = level_table.shape[1]
    span_bits = width.bit_length() - 1
    seq_count = lax.axis_size("seq")
    seq_bits = seq_count.bit_length() - 1
    position = lax.axis_index("seq")
    whole_x = lax.all_gather(tokens_x, "head", axis=1, tiled=True)
    onehot = (
        level_bins[:, :, None] == jnp.arange(bins_count, dtype=jnp.int32)[None, None, :]
    ).astype(jnp.float32)
    weight = jnp.einsum("thb,hbl->thl", onehot, level_table, precision=HIGH)
    levels = jnp.asarray(level_map(width))

    def one_head(pieces):
        grad_piece, val_piece, key_piece, weight_piece = pieces
        scores = jnp.einsum("td,sd->ts", grad_piece, val_piece, precision=HIGH)
        mixing = jnp.zeros_like(scores)
        for level in range(span_bits + 1):
            column = weight_piece[:, level][:, None]
            mixing = mixing + jnp.where(levels == level, column, 0.0)
        return jnp.dot(scores * mixing, key_piece, precision=HIGH)

    by_head = lax.map(
        one_head,
        (
            jnp.transpose(grad_out, (1, 0, 2)),
            jnp.transpose(values, (1, 0, 2)),
            jnp.transpose(keys, (1, 0, 2)),
            jnp.transpose(weight, (1, 0, 2)),
        ),
    )
    grad_query = jnp.transpose(by_head, (1, 0, 2))
    state = jnp.einsum("thd,the->hde", keys, values, precision=HIGH)
    bit_ids = jnp.arange(seq_bits, dtype=jnp.int32)[:, None]
    piece = lax.all_gather(state[None], "seq", axis=0, tiled=True)
    owners = jnp.arange(piece.shape[0], dtype=jnp.int32)[None, :]
    same_top = owners >> bit_ids + 1 == position >> bit_ids + 1
    owner_clear = owners >> bit_ids & 1 == 0
    mine_set = position >> bit_ids & 1 == 1
    select = (same_top & owner_clear & mine_set).astype(jnp.float32)
    buckets = jnp.einsum("bm,mhde->bhde", select, piece, precision=HIGH)
    for place in range(seq_bits):
        factor = weight[:, :, span_bits + 1 + place][:, :, None]
        grad_query = grad_query + factor * read_state(buckets[place], grad_out)
    flat = grad_query.reshape(width, local_heads * head_size)
    grad_wq = lax.psum_scatter(
        jnp.einsum("tc,tf->cf", whole_x, flat, precision=HIGH),
        "seq",
        scatter_dimension=0,
        tiled=True,
    )
    return (grad_query, grad_wq)


def solution(mesh):
    in_specs = (
        P("seq", "head"),
        P("seq", "head", None),
        P("seq", "head", None),
        P("seq", "head", None),
        P("head", None, None),
        P("seq", "head"),
    )
    out_specs = (P("seq", "head", None), P("seq", "head"))
    return jax.shard_map(body, mesh=mesh, in_specs=in_specs, out_specs=out_specs, check_vma=False)
```

profile of v0, /device:TPU:64, one launch (start us, length us, event | category | flops | bytes accessed | tf_op | source)
XLA Modules:
  0.0 431.9 jit_solution(8346400546764157606)
XLA Ops:
  7.2 12.0 %fusion.58 = f32[8,128,128]{2,1,0:T(8,128)} fusion(f32[1024,8,128]{2,1,0:T(8,128)} %param.10, f32[1024,8,128]{2,1,0:T(8,128)} %param.11), kind=kOutput, calls=%fused_computation.61 | convolution fusion | flops 1610612736 | bytes 8912896 | tf_op jit(solution)/shard_map/thd,the->hde/dot_general | solution.py:57
  20.3 5.2 %copy.99 = f32[1024,8,128]{2,0,1:T(8,128)} copy(f32[1024,8,128]{2,1,0:T(8,128)} %param.12) | data formatting | bytes 8388608 | tf_op args[3]
  26.3 5.0 %copy_bitcast_fusion = (f32[8,1024,128]{2,1,0:T(8,128)}, f32[8,1024,128]{2,1,0:T(8,128)}) fusion(f32[1024,8,128]{2,1,0:T(8,128)S(1)} %copy-done.3, f32[1024,8,128]{2,1,0:T(8,128)S(1)} %copy-done.4), kind=kLoop, calls=%fused_computation.63 | loop fusion | bytes 16777216 | tf_op jit(solution)/shard_map/transpose | solution.py:52
  31.3 154.4 %while.11 = (s32[]{:T(128)}, f32[8,1024,128]{1,2,0:T(8,128)}, f32[8,1024,128]{2,1,0:T(8,128)}, f32[8,1024,128]{2,1,0:T(8,128)}, f32[8,1024,17]{1,2,0:T(8,128)S(1...) while((s32[]{:T(128)}, f32[8,1024,128]{1,2,0:T(8,128)}, ...), condition=%wide.region_1.2_spmd.clone, body=%wide.region_0.1_spmd.sunk.clone.sunk | while | flops 3244294144 | bytes 43268412 | solution.py:47
  31.3 4.9 %fusion.108 = f32[1024,1024]{1,0:T(8,128)S(1)} fusion(f32[8,1024,128]{2,1,0:T(8,128)} %get-tuple-element.214, s32[]{:T(128)S(6)} %copy.104, f32[8,1024,128]{2,1,0:T(8,128)} %get-tuple-element.213), kind=kOutput, calls=%fused_computation.38.clone.1 | convolution fusion | flops 1610612736 | bytes 5243904 | tf_op jit(solution)/shard_map/while/body/eval_jaxpr/td,sd->ts/dot_general | solution.py:40
  36.4 14.2 %fusion.110 = f32[8,1024,128]{1,2,0:T(8,128)} fusion(f32[8,1024,128]{1,2,0:T(8,128)} %get-tuple-element.194, s32[]{:T(128)S(6)} %copy.104, f32[1024,1024]{1,0:T(8,128)S(1)} %fusion.108, pred[1024,1024]{1,0:T(32,128)(4,1)S(1)} %get-tuple-element.218, pred[1024,1024]{1,0:T(32,128)(4,1)S(1)} %copy-done.7, pred[1024,1024]{1,0:T(32,128)(4,1)S(1)} %copy-done.8, ...), kind=kOutput, calls=%fused_computation.36.clone.1 | convolution fusion | flops 1633681408 | bytes 16823296 | tf_op jit(solution)/shard_map/while/body/eval_jaxpr/dot_general | solution.py:45
  50.6 4.9 %fusion.108 = f32[1024,1024]{1,0:T(8,128)S(1)} fusion(f32[8,1024,128]{2,1,0:T(8,128)} %get-tuple-element.214, s32[]{:T(128)S(6)} %copy.104, f32[8,1024,128]{2,1,0:T(8,128)} %get-tuple-element.213), kind=kOutput, calls=%fused_computation.38.clone.1 | convolution fusion | flops 1610612736 | bytes 5243904 | tf_op jit(solution)/shard_map/while/body/eval_jaxpr/td,sd->ts/dot_general | solution.py:40
  55.6 14.2 %fusion.110 = f32[8,1024,128]{1,2,0:T(8,128)} fusion(f32[8,1024,128]{1,2,0:T(8,128)} %get-tuple-element.194, s32[]{:T(128)S(6)} %copy.104, f32[1024,1024]{1,0:T(8,128)S(1)} %fusion.108, pred[1024,1024]{1,0:T(32,128)(4,1)S(1)} %get-tuple-element.218, pred[1024,1024]{1,0:T(32,128)(4,1)S(1)} %copy-done.7, pred[1024,1024]{1,0:T(32,128)(4,1)S(1)} %copy-done.8, ...), kind=kOutput, calls=%fused_computation.36.clone.1 | convolution fusion | flops 1633681408 | bytes 16823296 | tf_op jit(solution)/shard_map/while/body/eval_jaxpr/dot_general | solution.py:45
  69.8 4.9 %fusion.108 = f32[1024,1024]{1,0:T(8,128)S(1)} fusion(f32[8,1024,128]{2,1,0:T(8,128)} %get-tuple-element.214, s32[]{:T(128)S(6)} %copy.104, f32[8,1024,128]{2,1,0:T(8,128)} %get-tuple-element.213), kind=kOutput, calls=%fused_computation.38.clone.1 | convolution fusion | flops 1610612736 | bytes 5243904 | tf_op jit(solution)/shard_map/while/body/eval_jaxpr/td,sd->ts/dot_general | solution.py:40
  74.9 14.3 %fusion.110 = f32[8,1024,128]{1,2,0:T(8,128)} fusion(f32[8,1024,128]{1,2,0:T(8,128)} %get-tuple-element.194, s32[]{:T(128)S(6)} %copy.104, f32[1024,1024]{1,0:T(8,128)S(1)} %fusion.108, pred[1024,1024]{1,0:T(32,128)(4,1)S(1)} %get-tuple-element.218, pred[1024,1024]{1,0:T(32,128)(4,1)S(1)} %copy-done.7, pred[1024,1024]{1,0:T(32,128)(4,1)S(1)} %copy-done.8, ...), kind=kOutput, calls=%fused_computation.36.clone.1 | convolution fusion | flops 1633681408 | bytes 16823296 | tf_op jit(solution)/shard_map/while/body/eval_jaxpr/dot_general | solution.py:45
  89.3 4.9 %fusion.108 = f32[1024,1024]{1,0:T(8,128)S(1)} fusion(f32[8,1024,128]{2,1,0:T(8,128)} %get-tuple-element.214, s32[]{:T(128)S(6)} %copy.104, f32[8,1024,128]{2,1,0:T(8,128)} %get-tuple-element.213), kind=kOutput, calls=%fused_computation.38.clone.1 | convolution fusion | flops 1610612736 | bytes 5243904 | tf_op jit(solution)/shard_map/while/body/eval_jaxpr/td,sd->ts/dot_general | solution.py:40
  94.3 14.2 %fusion.110 = f32[8,1024,128]{1,2,0:T(8,128)} fusion(f32[8,1024,128]{1,2,0:T(8,128)} %get-tuple-element.194, s32[]{:T(128)S(6)} %copy.104, f32[1024,1024]{1,0:T(8,128)S(1)} %fusion.108, pred[1024,1024]{1,0:T(32,128)(4,1)S(1)} %get-tuple-element.218, pred[1024,1024]{1,0:T(32,128)(4,1)S(1)} %copy-done.7, pred[1024,1024]{1,0:T(32,128)(4,1)S(1)} %copy-done.8, ...), kind=kOutput, calls=%fused_computation.36.clone.1 | convolution fusion | flops 1633681408 | bytes 16823296 | tf_op jit(solution)/shard_map/while/body/eval_jaxpr/dot_general | solution.py:45
  108.5 5.0 %fusion.108 = f32[1024,1024]{1,0:T(8,128)S(1)} fusion(f32[8,1024,128]{2,1,0:T(8,128)} %get-tuple-element.214, s32[]{:T(128)S(6)} %copy.104, f32[8,1024,128]{2,1,0:T(8,128)} %get-tuple-element.213), kind=kOutput, calls=%fused_computation.38.clone.1 | convolution fusion | flops 1610612736 | bytes 5243904 | tf_op jit(solution)/shard_map/while/body/eval_jaxpr/td,sd->ts/dot_general | solution.py:40
  113.6 14.4 %fusion.110 = f32[8,1024,128]{1,2,0:T(8,128)} fusion(f32[8,1024,128]{1,2,0:T(8,128)} %get-tuple-element.194, s32[]{:T(128)S(6)} %copy.104, f32[1024,1024]{1,0:T(8,128)S(1)} %fusion.108, pred[1024,1024]{1,0:T(32,128)(4,1)S(1)} %get-tuple-element.218, pred[1024,1024]{1,0:T(32,128)(4,1)S(1)} %copy-done.7, pred[1024,1024]{1,0:T(32,128)(4,1)S(1)} %copy-done.8, ...), kind=kOutput, calls=%fused_computation.36.clone.1 | convolution fusion | flops 1633681408 | bytes 16823296 | tf_op jit(solution)/shard_map/while/body/eval_jaxpr/dot_general | solution.py:45
  128.1 4.9 %fusion.108 = f32[1024,1024]{1,0:T(8,128)S(1)} fusion(f32[8,1024,128]{2,1,0:T(8,128)} %get-tuple-element.214, s32[]{:T(128)S(6)} %copy.104, f32[8,1024,128]{2,1,0:T(8,128)} %get-tuple-element.213), kind=kOutput, calls=%fused_computation.38.clone.1 | convolution fusion | flops 1610612736 | bytes 5243904 | tf_op jit(solution)/shard_map/while/body/eval_jaxpr/td,sd->ts/dot_general | solution.py:40
  133.1 14.1 %fusion.110 = f32[8,1024,128]{1,2,0:T(8,128)} fusion(f32[8,1024,128]{1,2,0:T(8,128)} %get-tuple-element.194, s32[]{:T(128)S(6)} %copy.104, f32[1024,1024]{1,0:T(8,128)S(1)} %fusion.108, pred[1024,1024]{1,0:T(32,128)(4,1)S(1)} %get-tuple-element.218, pred[1024,1024]{1,0:T(32,128)(4,1)S(1)} %copy-done.7, pred[1024,1024]{1,0:T(32,128)(4,1)S(1)} %copy-done.8, ...), kind=kOutput, calls=%fused_computation.36.clone.1 | convolution fusion | flops 1633681408 | bytes 16823296 | tf_op jit(solution)/shard_map/while/body/eval_jaxpr/dot_general | solution.py:45
  147.3 4.9 %fusion.108 = f32[1024,1024]{1,0:T(8,128)S(1)} fusion(f32[8,1024,128]{2,1,0:T(8,128)} %get-tuple-element.214, s32[]{:T(128)S(6)} %copy.104, f32[8,1024,128]{2,1,0:T(8,128)} %get-tuple-element.213), kind=kOutput, calls=%fused_computation.38.clone.1 | convolution fusion | flops 1610612736 | bytes 5243904 | tf_op jit(solution)/shard_map/while/body/eval_jaxpr/td,sd->ts/dot_general | solution.py:40
  152.3 14.2 %fusion.110 = f32[8,1024,128]{1,2,0:T(8,128)} fusion(f32[8,1024,128]{1,2,0:T(8,128)} %get-tuple-element.194, s32[]{:T(128)S(6)} %copy.104, f32[1024,1024]{1,0:T(8,128)S(1)} %fusion.108, pred[1024,1024]{1,0:T(32,128)(4,1)S(1)} %get-tuple-element.218, pred[1024,1024]{1,0:T(32,128)(4,1)S(1)} %copy-done.7, pred[1024,1024]{1,0:T(32,128)(4,1)S(1)} %copy-done.8, ...), kind=kOutput, calls=%fused_computation.36.clone.1 | convolution fusion | flops 1633681408 | bytes 16823296 | tf_op jit(solution)/shard_map/while/body/eval_jaxpr/dot_general | solution.py:45
  166.5 4.9 %fusion.108 = f32[1024,1024]{1,0:T(8,128)S(1)} fusion(f32[8,1024,128]{2,1,0:T(8,128)} %get-tuple-element.214, s32[]{:T(128)S(6)} %copy.104, f32[8,1024,128]{2,1,0:T(8,128)} %get-tuple-element.213), kind=kOutput, calls=%fused_computation.38.clone.1 | convolution fusion | flops 1610612736 | bytes 5243904 | tf_op jit(solution)/shard_map/while/body/eval_jaxpr/td,sd->ts/dot_general | solution.py:40
  171.5 14.2 %fusion.110 = f32[8,1024,128]{1,2,0:T(8,128)} fusion(f32[8,1024,128]{1,2,0:T(8,128)} %get-tuple-element.194, s32[]{:T(128)S(6)} %copy.104, f32[1024,1024]{1,0:T(8,128)S(1)} %fusion.108, pred[1024,1024]{1,0:T(32,128)(4,1)S(1)} %get-tuple-element.218, pred[1024,1024]{1,0:T(32,128)(4,1)S(1)} %copy-done.7, pred[1024,1024]{1,0:T(32,128)(4,1)S(1)} %copy-done.8, ...), kind=kOutput, calls=%fused_computation.36.clone.1 | convolution fusion | flops 1633681408 | bytes 16823296 | tf_op jit(solution)/shard_map/while/body/eval_jaxpr/dot_general | solution.py:45
  185.7 20.2 %fusion.51 = f32[5,8,128,128]{3,0,2,1:T(8,128)S(1)} fusion(f32[32,8,128,128]{3,2,1,0:T(8,128)} %bitcast.130, s32[5]{0:T(128)S(1)} %get-tuple-element.109, s32[5]{0:T(128)S(1)} %get-tuple-element.108, pred[5]{0:T(512)(128)(4,1)S(1)} %and_compare_fusion.1), kind=kOutput, calls=%fused_computation.48 | convolution fusion | flops 251659360 | bytes 19398700 | tf_op jit(solution)/shard_map/bm,mhde->bhde/dot_general | solution.py:65
  206.0 2.7 fusion.87
  208.7 4.6 %fusion.61 = f32[8,128,1024]{2,1,0:T(8,128)S(1)} fusion(f32[8,128,128]{2,1,0:T(8,128)S(1)} %bitcast.138, f32[1024,8,128]{2,1,0:T(8,128)S(1)} %copy-done.2), kind=kOutput, calls=%fused_computation.66 | convolution fusion | flops 1610612736 | bytes 8912896 | tf_op jit(solution)/shard_map/hde,the->thd/dot_general | solution.py:21
  213.3 4.6 %fusion.63 = f32[8,128,1024]{2,1,0:T(8,128)S(1)} fusion(f32[8,128,128]{2,1,0:T(8,128)S(1)} %bitcast.137, f32[1024,8,128]{2,1,0:T(8,128)S(1)} %copy-done.2), kind=kOutput, calls=%fused_computation.68 | convolution fusion | flops 1610612736 | bytes 8912896 | tf_op jit(solution)/shard_map/hde,the->thd/dot_general | solution.py:21
  217.8 4.7 %fusion.65 = f32[8,128,1024]{2,1,0:T(8,128)S(1)} fusion(f32[8,128,128]{2,1,0:T(8,128)S(1)} %bitcast.136, f32[1024,8,128]{2,1,0:T(8,128)S(1)} %copy-done.2), kind=kOutput, calls=%fused_computation.70 | convolution fusion | flops 1610612736 | bytes 8912896 | tf_op jit(solution)/shard_map/hde,the->thd/dot_general | solution.py:21
  222.6 5.6 %fusion.67 = f32[8,128,1024]{2,1,0:T(8,128)} fusion(f32[8,128,128]{2,1,0:T(8,128)S(1)} %bitcast.135, f32[1024,8,128]{2,1,0:T(8,128)S(1)} %copy-done.2), kind=kOutput, calls=%fused_computation.72 | convolution fusion | flops 1610612736 | bytes 8912896 | tf_op jit(solution)/shard_map/hde,the->thd/dot_general | solution.py:21
  228.2 9.8 %fusion.53 = f32[1024,8,128]{0,2,1:T(8,128)} fusion(f32[8,128,1024]{2,1,0:T(8,128)S(1)} %fusion.61, f32[8,128,1024]{2,1,0:T(8,128)S(1)} %fusion.63, f32[8,128,1024]{2,1,0:T(8,128)S(1)} %fusion.65, f32[8,128,1024]{2,1,0:T(8,128)} %fusion.67, f32[8,1024,128]{1,2,0:T(8,128)} %get-tuple-element.39, f32[8,128,128]{2,1,0:T(8,128)S(1)} %bitcast.134, ...), kind=kOutput, calls=%fused_computation.52 | convolution fusion | flops 1621098496 | bytes 30048256 | tf_op jit(solution)/shard_map/hde,the->thd/dot_general | solution.py:21
  238.0 10.8 %all-gather.4.cloned.1.call-done = f32[1024,4096]{1,0:T(8,128)} async-done(((f32[1024,1024]{1,0:T(8,128)}), f32[1024,4096]{1,0:T(8,128)}) %all-gather.4.cloned.1.call-update) | async-done | bytes 16777232 | tf_op jit(solution)/shard_map/all_gather | solution.py:31
  248.8 58.5 %convolution_bitcast_fusion = f32[4096,1024]{0,1:T(8,128)} fusion(f32[1024,1024]{0,1:T(8,128)} %bitcast.131, f32[1024,4096]{1,0:T(8,128)} %all-gather.4.cloned.1.call-done), kind=kOutput, calls=%fused_computation.50 | convolution fusion | flops 51539607552 | bytes 37748736 | tf_op jit(solution)/shard_map/tc,tf->cf/dot_general | solution.py:71
  307.3 5.4 %copy.63 = f32[1024,8,128]{2,1,0:T(8,128)} copy(f32[1024,8,128]{0,2,1:T(8,128)} %fusion.53) | data formatting | bytes 8388608
  312.7 110.5 %reduce-scatter.2.cloned.1.call-done = f32[128,1024]{0,1:T(8,128)} async-done(((f32[4096,1024]{0,1:T(8,128)}), f32[128,1024]{0,1:T(8,128)}) %reduce-scatter.2.cloned.1.call-update) | async-done | bytes 524304 | tf_op jit(solution)/shard_map/reduce_scatter | solution.py:70
  423.2 2.0 copy.64
  (125 shorter events, 2.4 us)
Async XLA Ops:
  7.2 18.3 %copy-start = (f32[8,16,17]{2,1,0:T(8,128)S(1)}, f32[8,16,17]{2,1,0:T(8,128)}, u32[]{:S(2)}) copy-start(f32[8,16,17]{2,1,0:T(8,128)} %param.13) | copy-start | bytes 26116
  7.2 178.6 %all-gather.6.cloned.1.call-start = ((), (), s32[]{:S(2)}) async-start(), calls=%async_computation.3 | async-start | bytes 17301504 | tf_op jit(solution)/shard_map/all_gather | solution.py:59
  19.3 229.5 %all-gather.4.cloned.1.call-start = ((), (), s32[]{:S(2)}) async-start(), calls=%async_computation.1 | async-start | bytes 20971520 | tf_op jit(solution)/shard_map/all_gather | solution.py:31
  19.3 6.2 %copy-start.5 = (s32[1024,8]{0,1:T(8,128)S(1)}, s32[1024,8]{0,1:T(8,128)}, u32[]{:S(2)}) copy-start(s32[1024,8]{0,1:T(8,128)} %param.14) | copy-start | bytes 98308
  20.0 403.1 %reduce-scatter.2.cloned.1.call-start = ((), (), s32[]{:S(2)}) async-start(), calls=%async_computation.2 | async-start | bytes 17301504 | tf_op jit(solution)/shard_map/reduce_scatter | solution.py:70
  20.2 6.0 %copy-start.3 = (f32[1024,8,128]{2,1,0:T(8,128)S(1)}, f32[1024,8,128]{2,1,0:T(8,128)}, u32[]{:S(2)}) copy-start(f32[1024,8,128]{2,1,0:T(8,128)} %param.10) | copy-start | bytes 12582916
  20.3 6.0 %copy-start.4 = (f32[1024,8,128]{2,1,0:T(8,128)S(1)}, f32[1024,8,128]{2,1,0:T(8,128)}, u32[]{:S(2)}) copy-start(f32[1024,8,128]{2,1,0:T(8,128)} %param.11) | copy-start | bytes 12582916
  31.3 5.0 %copy-start.7 = (pred[1024,1024]{1,0:T(32,128)(4,1)S(1)}, pred[1024,1024]{1,0:T(32,128)(4,1)}, u32[]{:S(2)}) copy-start(pred[1024,1024]{1,0:T(32,128)(4,1)} %get-tuple-element.219) | copy-start | bytes 3145732 | tf_op jit(solution)/shard_map/while
  31.3 5.0 %copy-start.8 = (pred[1024,1024]{1,0:T(32,128)(4,1)S(1)}, pred[1024,1024]{1,0:T(32,128)(4,1)}, u32[]{:S(2)}) copy-start(pred[1024,1024]{1,0:T(32,128)(4,1)} %get-tuple-element.220) | copy-start | bytes 3145732 | tf_op jit(solution)/shard_map/while
  31.3 5.0 %copy-start.9 = (pred[1024,1024]{1,0:T(32,128)(4,1)S(1)}, pred[1024,1024]{1,0:T(32,128)(4,1)}, u32[]{:S(2)}) copy-start(pred[1024,1024]{1,0:T(32,128)(4,1)} %get-tuple-element.221) | copy-start | bytes 3145732 | tf_op jit(solution)/shard_map/while
  31.3 5.0 %copy-start.10 = (pred[1024,1024]{1,0:T(32,128)(4,1)S(1)}, pred[1024,1024]{1,0:T(32,128)(4,1)}, u32[]{:S(2)}) copy-start(pred[1024,1024]{1,0:T(32,128)(4,1)} %get-tuple-element.222) | copy-start | bytes 3145732 | tf_op jit(solution)/shard_map/while
  31.3 5.0 %copy-start.11 = (pred[1024,1024]{1,0:T(32,128)(4,1)S(1)}, pred[1024,1024]{1,0:T(32,128)(4,1)}, u32[]{:S(2)}) copy-start(pred[1024,1024]{1,0:T(32,128)(4,1)} %get-tuple-element.223) | copy-start | bytes 3145732 | tf_op jit(solution)/shard_map/while
  69.8 5.0 %copy-start.7 = (pred[1024,1024]{1,0:T(32,128)(4,1)S(1)}, pred[1024,1024]{1,0:T(32,128)(4,1)}, u32[]{:S(2)}) copy-start(pred[1024,1024]{1,0:T(32,128)(4,1)} %get-tuple-element.219) | copy-start | bytes 3145732 | tf_op jit(solution)/shard_map/while
  69.8 5.1 %copy-start.8 = (pred[1024,1024]{1,0:T(32,128)(4,1)S(1)}, pred[1024,1024]{1,0:T(32,128)(4,1)}, u32[]{:S(2)}) copy-start(pred[1024,1024]{1,0:T(32,128)(4,1)} %get-tuple-element.220) | copy-start | bytes 3145732 | tf_op jit(solution)/shard_map/while
  69.8 5.1 %copy-start.9 = (pred[1024,1024]{1,0:T(32,128)(4,1)S(1)}, pred[1024,1024]{1,0:T(32,128)(4,1)}, u32[]{:S(2)}) copy-start(pred[1024,1024]{1,0:T(32,128)(4,1)} %get-tuple-element.221) | copy-start | bytes 3145732 | tf_op jit(solution)/shard_map/while
  69.8 5.1 %copy-start.10 = (pred[1024,1024]{1,0:T(32,128)(4,1)S(1)}, pred[1024,1024]{1,0:T(32,128)(4,1)}, u32[]{:S(2)}) copy-start(pred[1024,1024]{1,0:T(32,128)(4,1)} %get-tuple-element.222) | copy-start | bytes 3145732 | tf_op jit(solution)/shard_map/while
  69.8 5.1 %copy-start.11 = (pred[1024,1024]{1,0:T(32,128)(4,1)S(1)}, pred[1024,1024]{1,0:T(32,128)(4,1)}, u32[]{:S(2)}) copy-start(pred[1024,1024]{1,0:T(32,128)(4,1)} %get-tuple-element.223) | copy-start | bytes 3145732 | tf_op jit(solution)/shard_map/while
  89.2 5.0 %copy-start.7 = (pred[1024,1024]{1,0:T(32,128)(4,1)S(1)}, pred[1024,1024]{1,0:T(32,128)(4,1)}, u32[]{:S(2)}) copy-start(pred[1024,1024]{1,0:T(32,128)(4,1)} %get-tuple-element.219) | copy-start | bytes 3145732 | tf_op jit(solution)/shard_map/while
  89.2 5.0 %copy-start.8 = (pred[1024,1024]{1,0:T(32,128)(4,1)S(1)}, pred[1024,1024]{1,0:T(32,128)(4,1)}, u32[]{:S(2)}) copy-start(pred[1024,1024]{1,0:T(32,128)(4,1)} %get-tuple-element.220) | copy-start | bytes 3145732 | tf_op jit(solution)/shard_map/while
  89.2 5.0 %copy-start.9 = (pred[1024,1024]{1,0:T(32,128)(4,1)S(1)}, pred[1024,1024]{1,0:T(32,128)(4,1)}, u32[]{:S(2)}) copy-start(pred[1024,1024]{1,0:T(32,128)(4,1)} %get-tuple-element.221) | copy-start | bytes 3145732 | tf_op jit(solution)/shard_map/while
  89.2 5.0 %copy-start.10 = (pred[1024,1024]{1,0:T(32,128)(4,1)S(1)}, pred[1024,1024]{1,0:T(32,128)(4,1)}, u32[]{:S(2)}) copy-start(pred[1024,1024]{1,0:T(32,128)(4,1)} %get-tuple-element.222) | copy-start | bytes 3145732 | tf_op jit(solution)/shard_map/while
  89.3 5.0 %copy-start.11 = (pred[1024,1024]{1,0:T(32,128)(4,1)S(1)}, pred[1024,1024]{1,0:T(32,128)(4,1)}, u32[]{:S(2)}) copy-start(pred[1024,1024]{1,0:T(32,128)(4,1)} %get-tuple-element.223) | copy-start | bytes 3145732 | tf_op jit(solution)/shard_map/while
  108.5 5.1 %copy-start.7 = (pred[1024,1024]{1,0:T(32,128)(4,1)S(1)}, pred[1024,1024]{1,0:T(32,128)(4,1)}, u32[]{:S(2)}) copy-start(pred[1024,1024]{1,0:T(32,128)(4,1)} %get-tuple-element.219) | copy-start | bytes 3145732 | tf_op jit(solution)/shard_map/while
  108.5 5.1 %copy-start.8 = (pred[1024,1024]{1,0:T(32,128)(4,1)S(1)}, pred[1024,1024]{1,0:T(32,128)(4,1)}, u32[]{:S(2)}) copy-start(pred[1024,1024]{1,0:T(32,128)(4,1)} %get-tuple-element.220) | copy-start | bytes 3145732 | tf_op jit(solution)/shard_map/while
  108.5 5.1 %copy-start.9 = (pred[1024,1024]{1,0:T(32,128)(4,1)S(1)}, pred[1024,1024]{1,0:T(32,128)(4,1)}, u32[]{:S(2)}) copy-start(pred[1024,1024]{1,0:T(32,128)(4,1)} %get-tuple-element.221) | copy-start | bytes 3145732 | tf_op jit(solution)/shard_map/while
  108.5 5.1 %copy-start.10 = (pred[1024,1024]{1,0:T(32,128)(4,1)S(1)}, pred[1024,1024]{1,0:T(32,128)(4,1)}, u32[]{:S(2)}) copy-start(pred[1024,1024]{1,0:T(32,128)(4,1)} %get-tuple-element.222) | copy-start | bytes 3145732 | tf_op jit(solution)/shard_map/while
  108.5 5.1 %copy-start.11 = (pred[1024,1024]{1,0:T(32,128)(4,1)S(1)}, pred[1024,1024]{1,0:T(32,128)(4,1)}, u32[]{:S(2)}) copy-start(pred[1024,1024]{1,0:T(32,128)(4,1)} %get-tuple-element.223) | copy-start | bytes 3145732 | tf_op jit(solution)/shard_map/while
  128.0 5.0 %copy-start.8 = (pred[1024,1024]{1,0:T(32,128)(4,1)S(1)}, pred[1024,1024]{1,0:T(32,128)(4,1)}, u32[]{:S(2)}) copy-start(pred[1024,1024]{1,0:T(32,128)(4,1)} %get-tuple-element.220) | copy-start | bytes 3145732 | tf_op jit(solution)/shard_map/while
  128.1 5.0 %copy-start.9 = (pred[1024,1024]{1,0:T(32,128)(4,1)S(1)}, pred[1024,1024]{1,0:T(32,128)(4,1)}, u32[]{:S(2)}) copy-start(pred[1024,1024]{1,0:T(32,128)(4,1)} %get-tuple-element.221) | copy-start | bytes 3145732 | tf_op jit(solution)/shard_map/while
  128.1 5.0 %copy-start.10 = (pred[1024,1024]{1,0:T(32,128)(4,1)S(1)}, pred[1024,1024]{1,0:T(32,128)(4,1)}, u32[]{:S(2)}) copy-start(pred[1024,1024]{1,0:T(32,128)(4,1)} %get-tuple-element.222) | copy-start | bytes 3145732 | tf_op jit(solution)/shard_map/while
  128.1 5.0 %copy-start.11 = (pred[1024,1024]{1,0:T(32,128)(4,1)S(1)}, pred[1024,1024]{1,0:T(32,128)(4,1)}, u32[]{:S(2)}) copy-start(pred[1024,1024]{1,0:T(32,128)(4,1)} %get-tuple-element.223) | copy-start | bytes 3145732 | tf_op jit(solution)/shard_map/while
  307.3 117.9 %copy-start.1 = (f32[8,16,17]{2,1,0:T(8,128)S(1)}, f32[8,16,17]{2,1,0:T(8,128)}, u32[]{:S(2)}) copy-start(f32[8,16,17]{2,1,0:T(8,128)} %param.13) | copy-start | bytes 26116
  (18 other events, 87.6 us)
Sparse Core Ops, SparseCore 0:
  19.4 73.6 all-gather.5
  94.8 153.9 all-gather.3
  307.4 115.6 reduce-scatter.1
where the time goes:
time: 440 us; the launch traced here: 432 us
  matrix products  274 us (62%)
  waiting for transfers between devices  122 us (28%)
  local copies, waits for them, and re-layouts  21.2 us (5%)
  between operations  14.1 us (3%)
    dot_general x8, matrix products, one_head(): return jnp.dot(scores * mixing, key_piece, precision=HIGH)  114 us
    reduce_scatter x1, waiting for transfers between devices, body(): lax.psum_scatter(jnp.einsum('tc,tf->cf', whole_x, flat, precision=HIGH),...  110 us
    dot_general x1, matrix products, body(): jnp.einsum('tc,tf->cf', whole_x, flat, precision=HIGH)  58.5 us
    dot_general x8, matrix products, one_head(): scores = jnp.einsum('td,sd->ts', grad_piece, val_piece, precision=HIGH)  39.2 us
    dot_general x5, matrix products, read_state(): return jnp.einsum('hde,the->thd', state, grad_out, precision=HIGH)  29.3 us
    dot_general x1, matrix products, body(): buckets = jnp.einsum('bm,mhde->bhde', select, piece, precision=HIGH)  20.2 us
    unnamed x20, local copies, waits for them, and re-layouts  12.8 us
    dot_general x1, matrix products, body(): state = jnp.einsum('thd,the->hde', keys, values, precision=HIGH)  12 us
  transfers between devices with their start and end apart: 3, of which 2 were waited for; matrix products, arithmetic and copies ran while one was open for 51% of the time, Pallas kernels for 0%

commit v1 on v0

v1 whole, which is shorter than its diff:
```python
import jax
import jax.numpy as jnp
from jax import lax
from jax.experimental import pallas as pl
from jax.experimental.pallas import tpu as pltpu
from jax.sharding import PartitionSpec as P

MESH = pl.DeviceIdType.MESH
F32 = jnp.float32
BF16 = jnp.bfloat16
NT = (((1,), (1,)), ((), ()))
NN = (((1,), (0,)), ((), ()))


def split(a):
    high = a.astype(BF16)
    return high, (a - high.astype(F32)).astype(BF16)


def mm(a, b, dims=NN):
    return lax.dot_general(a, b, dims, preferred_element_type=F32)


def kernel(
    x_hbm, k_hbm, v_hbm, g_hbm, tab_ref, bins_ref,
    gq_hbm, wq_ref,
    xbuf, kv, gbuf, oq, gt_hi, gt_lo, wts, lev, chunk_st, state, bucket,
    core_in, y_in, z_in, x_hi, x_lo,
    load_sem, out_sem, own_sem, xs, xr, bs, br, ss, sr, cs, cr, ys, yr, zs, zr,
):
    tokens, width = x_hbm.shape
    heads = tab_ref.shape[0]
    hd = 128
    feats = heads * hd
    quarter = tokens // 4
    half_t = tokens // 2
    half_f = feats // 2
    half_h = heads // 2
    span_bits = tokens.bit_length() - 1
    tile = min(256, feats)

    seq = lax.axis_index("seq")
    h = lax.axis_index("head")
    z, y, core = seq // 8, (seq // 2) % 4, seq % 2

    def at(zz, yy, cc):
        return zz * 8 + yy * 2 + cc

    y_up, y_down = (y + 1) % 4, (y + 3) % 4
    z_up, z_down = (z + 1) % 4, (z + 3) % 4
    h_up, h_down = (h + 1) % 4, (h + 3) % 4
    mate = (at(z, y, 1 - core), h)
    to_y_up, to_y_down = (at(z, y_up, core), h), (at(z, y_down, core), h)
    to_z_up, to_z_down = (at(z_up, y, core), h), (at(z_down, y, core), h)
    to_h_up, to_h_down = (seq, h_up), (seq, h_down)
    y_flip = y + 1 - 2 * (y % 2)
    z_flip = z + 1 - 2 * (z % 2)
    y_far, z_far = (y + 2) % 4, (z + 2) % 4
    flips = [
        mate,
        (at(z, y_flip, core), h),
        (at(z, y_far, core), h),
        (at(z_flip, y, core), h),
        (at(z_far, y, core), h),
    ]
    friends = [
        mate, to_y_up, to_y_down, to_z_up, to_z_down, to_h_up, to_h_down, flips[2], flips[4],
    ]

    def rcopy(src, dst, ssem, rsem, dev):
        return pltpu.make_async_remote_copy(
            src_ref=src, dst_ref=dst, send_sem=ssem, recv_sem=rsem,
            device_id=dev, device_id_type=MESH,
        )

    loads = [
        pltpu.make_async_copy(v_hbm, kv.at[pl.ds(tokens * heads, tokens * heads)], load_sem.at[0]),
        pltpu.make_async_copy(k_hbm, kv.at[pl.ds(0, tokens * heads)], load_sem.at[1]),
        pltpu.make_async_copy(g_hbm, gbuf.at[pl.ds(0, tokens * heads)], load_sem.at[2]),
    ]
    for c in loads:
        c.start()

    barrier = pltpu.get_barrier_semaphore()
    for f in friends:
        pl.semaphore_signal(barrier, inc=1, device_id=f, device_id_type=MESH)
    pl.semaphore_wait(barrier, len(friends))

    offsets = (2, 1, 3, 0)

    def x_cols(j):
        yt = (y + offsets[j]) % 4
        return x_hbm.at[:, pl.ds(pl.multiple_of(yt * 256, 256), 256)]

    def x_own(j):
        return pltpu.make_async_copy(x_cols(j), xbuf.at[j], own_sem.at[j])

    def x_right(j):
        return rcopy(x_cols(j), xbuf.at[4 + 2 * j], xs.at[0, j], xr.at[0, j], to_h_up)

    def x_left(j):
        return rcopy(x_cols(j), xbuf.at[5 + 2 * j], xs.at[1, j], xr.at[1, j], to_h_down)

    low_t, high_t = pl.ds(0, half_t), pl.ds(half_t, half_t)

    def x_right2(j):
        return rcopy(
            xbuf.at[4 + 2 * j, low_t], xbuf.at[12 + j, low_t], xs.at[2, j], xr.at[2, j], to_h_up)

    def x_left2(j):
        return rcopy(
            xbuf.at[5 + 2 * j, high_t], xbuf.at[12 + j, high_t], xs.at[3, j], xr.at[3, j], to_h_down)

    for j in range(4):
        x_right(j).start()
        x_left(j).start()
    for j in range(4):
        x_own(j).start()

    loads[0].wait()
    loads[1].wait()

    def head_rows(hh, first=0):
        return pl.ds(first + hh, tokens, stride=heads)

    def states_of(hh, carry):
        kh = kv[head_rows(hh), :]
        vh = kv[head_rows(hh, tokens * heads), :]
        total = None
        for c in range(4):
            rows = slice(c * quarter, (c + 1) * quarter)
            k_hi, k_lo = split(kh[rows])
            v_hi, v_lo = split(vh[rows].T)
            both = mm(v_hi, jnp.concatenate([k_hi, k_lo], axis=1))
            st = both[:, :hd] + both[:, hd:] + mm(v_lo, k_hi)
            chunk_st[hh, c] = st
            total = st if total is None else total + st
        state[hh] = total
        return carry

    lax.fori_loop(0, heads, states_of, 0)

    mine_h = pl.ds(core * half_h, half_h)
    other_h = pl.ds((1 - core) * half_h, half_h)

    def climb(p):
        if p == 0:
            return rcopy(state, bucket.at[0], bs.at[0], br.at[0], mate)
        return rcopy(state.at[mine_h], bucket.at[p, mine_h], bs.at[p], br.at[p], flips[p])

    def share(p):
        return rcopy(bucket.at[p, mine_h], bucket.at[p, mine_h], ss.at[p], sr.at[p], mate)

    def share_in(p):
        return rcopy(bucket.at[p, other_h], bucket.at[p, other_h], ss.at[p], sr.at[p], mate)

    def pump(p):
        climb(p).wait_recv()
        if p > 0:
            share(p).start()
            share_in(p).wait_recv()
        climb(p).wait_send()
        if p < 4:
            state[...] = state[...] + bucket[p]
            climb(p + 1).start()

    climb(0).start()

    for hh in range(heads):
        row = bins_ref[hh:hh + 1, :]
        tab = tab_ref[hh]
        acc = jnp.zeros((tab.shape[0], tokens), F32)
        for b in range(tab.shape[1]):
            acc = acc + jnp.where(row == b, tab[:, b:b + 1], 0.0)
        wts[hh] = acc

    later = lax.broadcasted_iota(jnp.int32, (quarter, quarter), 0)
    earlier = lax.broadcasted_iota(jnp.int32, (quarter, quarter), 1)
    differ = later ^ earlier
    digits = jnp.zeros((quarter, quarter), jnp.int32)
    for place in range(span_bits - 2):
        digits = digits + jnp.where(differ >= (1 << place), 1, 0)
    lev[...] = jnp.where(earlier <= later, digits, -1)

    loads[2].wait()

    def local_of(hh, carry):
        kh = kv[head_rows(hh), :]
        vh = kv[head_rows(hh, tokens * heads), :]
        gh = gbuf[head_rows(hh), :]
        levels = lev[...]
        parts = []
        for c in range(4):
            rows = slice(c * quarter, (c + 1) * quarter)
            k_hi, k_lo = split(kh[rows])
            v_hi, v_lo = split(vh[rows])
            g_hi, g_lo = split(gh[rows])
            g_two = jnp.concatenate([g_hi, g_lo], axis=1)
            scores = mm(g_two, jnp.concatenate([v_hi, v_hi], axis=1), NT) + mm(g_hi, v_lo, NT)
            w = wts[hh, :, rows].T
            mix = jnp.zeros((quarter, quarter), F32)
            for level in range(span_bits - 1):
                mix = jnp.where(levels == level, w[:, level:level + 1], mix)
            m_hi, m_lo = split(scores * mix)
            both = mm(m_hi, jnp.concatenate([k_hi, k_lo], axis=1))
            out = both[:, :hd] + both[:, hd:] + mm(m_lo, k_hi)

            def read(st):
                s_hi, s_lo = split(st)
                return mm(g_two, jnp.concatenate([s_hi, s_hi], axis=0)) + mm(g_hi, s_lo)

            if c % 2:
                out = out + w[:, span_bits - 1:span_bits] * read(chunk_st[hh, c - 1])
            if c >= 2:
                out = out + w[:, span_bits:span_bits + 1] * read(chunk_st[hh, 0] + chunk_st[hh, 1])
            parts.append(out)
        oq[head_rows(hh), :] = jnp.concatenate(parts, axis=0)

        @pl.when(hh == heads // 4 - 1)
        def _():
            pump(0)

        @pl.when(hh == heads - 2)
        def _():
            pump(1)

        return carry

    if heads >= 4:
        lax.fori_loop(0, heads, local_of, 0)
    else:
        for hh in range(heads):
            local_of(hh, 0)
        pump(0)
        pump(1)

    bits = [core, y % 2, y // 2, z % 2, z // 2]

    def read_pair(p):
        on_a = jnp.where(bits[p] == 1, 1.0, 0.0).astype(F32)
        on_b = jnp.where(bits[p + 1] == 1, 1.0, 0.0).astype(F32)
        first = span_bits + 1 + p

        def step(hh, carry):
            g_hi, g_lo = split(gbuf[head_rows(hh), :])
            g_two = jnp.concatenate([g_hi, g_lo], axis=1)
            s_hi, s_lo = split(jnp.concatenate([bucket[p, hh] * on_a, bucket[p + 1, hh] * on_b], axis=1))
            got = mm(g_two, jnp.concatenate([s_hi, s_hi], axis=0)) + mm(g_hi, s_lo)
            w = wts[hh].T
            oq[head_rows(hh), :] = (
                oq[head_rows(hh), :]
                + w[:, first:first + 1] * got[:, :hd]
                + w[:, first + 1:first + 2] * got[:, hd:]
            )
            return carry

        lax.fori_loop(0, heads, step, 0)

    pump(2)
    read_pair(0)
    pump(3)
    read_pair(2)
    pump(4)

    on_last = jnp.where(bits[4] == 1, 1.0, 0.0).astype(F32)

    def finish_head(hh, carry):
        g_hi, g_lo = split(gbuf[head_rows(hh), :])
        g_two = jnp.concatenate([g_hi, g_lo], axis=1)
        s_hi, s_lo = split(bucket[4, hh] * on_last)
        got = mm(g_two, jnp.concatenate([s_hi, s_hi], axis=0)) + mm(g_hi, s_lo)
        last = span_bits + 5
        done = oq[head_rows(hh), :] + wts[hh].T[:, last:last + 1] * got
        oq[head_rows(hh), :] = done
        t_hi, t_lo = split(done.T)
        here = pl.ds(pl.multiple_of(hh * hd, hd), hd)
        gt_hi[here, :] = t_hi
        gt_lo[here, :] = t_lo
        return carry

    lax.fori_loop(0, heads, finish_head, 0)
    out_copy = pltpu.make_async_copy(oq, gq_hbm, out_sem)
    out_copy.start()

    low_f, high_f = pl.ds(0, half_f), pl.ds(half_f, half_f)

    def sums(m, part=None):
        first, count = (0, feats) if part is None else (part * half_f, half_f)
        return kv.at[pl.ds(pl.multiple_of(m * feats + first, 8), count)]

    def core_out(n):
        return gbuf.at[pl.ds(pl.multiple_of((n % 4) * feats, 8), feats)]

    def core_copy(n):
        return rcopy(core_out(n), core_in.at[n % 4], cs.at[n], cr.at[n], mate)

    y_far_lo, y_far_hi, y_near_up, y_near_down = 0, 1, 2, 3

    def y_copy(m, slot, kind):
        if kind == y_far_lo:
            src, dst, dev = sums(m, 0), y_in.at[slot, 0, low_f], to_y_up
        elif kind == y_far_hi:
            src, dst, dev = sums(m, 1), y_in.at[slot, 0, high_f], to_y_down
        elif kind == y_near_up:
            src, dst, dev = sums(m), y_in.at[slot, 1], to_y_up
        else:
            src, dst, dev = sums(m), y_in.at[slot, 2], to_y_down
        return rcopy(src, dst, ys.at[slot, kind], yr.at[slot, kind], dev)

    def z_copy(m, slot, kind):
        if kind == 0:
            src, dst, dev = sums(m, 0), z_in.at[slot, 0, low_f], to_z_up
        elif kind == 1:
            src, dst, dev = sums(m, 1), z_in.at[slot, 1, high_f], to_z_down
        elif kind == 2:
            src, dst, dev = sums(m), z_in.at[slot, 1], to_z_down
        else:
            src, dst, dev = sums(m), z_in.at[slot, 0], to_z_up
        return rcopy(src, dst, zs.at[slot, kind], zr.at[slot, kind], dev)

    last_unit = (3, 10, 11, 15)
    block_of = (h, h_down, h_up, (h + 2) % 4)

    def z_dist(slot):
        return (z + 4 - block_of[slot]) % 4

    def z_first(slot):
        m = last_unit[slot]

        @pl.when(z_dist(slot) == 2)
        def _():
            z_copy(m, slot, 0).start()
            z_copy(m, slot, 1).start()

    def z_middle(slot):
        m = last_unit[slot]

        @pl.when(z_dist(slot) == 1)
        def _():
            z_copy(m, slot, 1).wait_recv()
            s = sums(m, 1)
            s[...] = s[...] + z_in[slot, 1, half_f:, :]
            z_copy(m, slot, 2).start()

        @pl.when(z_dist(slot) == 3)
        def _():
            z_copy(m, slot, 0).wait_recv()
            s = sums(m, 0)
            s[...] = s[...] + z_in[slot, 0, :half_f, :]
            z_copy(m, slot, 3).start()

    def z_root(slot):
        m = last_unit[slot]

        @pl.when(z_dist(slot) == 0)
        def _():
            z_copy(m, slot, 2).wait_recv()
            z_copy(m, slot, 3).wait_recv()
            s = sums(m)
            wq_ref[...] = (s[...] + z_in[slot, 0] + z_in[slot, 1]).T

    def z_drain(slot):
        m = last_unit[slot]

        @pl.when(z_dist(slot) == 2)
        def _():
            z_copy(m, slot, 0).wait_send()
            z_copy(m, slot, 1).wait_send()

        @pl.when(z_dist(slot) == 1)
        def _():
            z_copy(m, slot, 2).wait_send()

        @pl.when(z_dist(slot) == 3)
        def _():
            z_copy(m, slot, 3).wait_send()

    def place(m):
        near = jnp.logical_and(m >= 4, m < 12)
        slot = jnp.where(m < 4, 0, jnp.where(m < 12, 1 + m % 2, 3))
        j = jnp.where(near, (m - 4) // 2, m % 4)
        return slot, j

    def settle(m):
        slot, j = place(m)
        core_copy(m).wait_recv()
        s = sums(m)
        s[...] = s[...] + core_in[m % 4]

        @pl.when(j == 0)
        def _():
            y_copy(m, slot, y_far_lo).start()
            y_copy(m, slot, y_far_hi).start()

        @pl.when(j == 1)
        def _():
            y_copy(m, slot, y_far_lo).wait_recv()
            t = sums(m, 0)
            t[...] = t[...] + y_in[slot, 0, :half_f, :]
            y_copy(m, slot, y_near_up).start()

        @pl.when(j == 2)
        def _():
            y_copy(m, slot, y_far_hi).wait_recv()
            t = sums(m, 1)
            t[...] = t[...] + y_in[slot, 0, half_f:, :]
            y_copy(m, slot, y_near_down).start()

        @pl.when(j == 3)
        def _():
            y_copy(m, slot, y_near_up).wait_recv()
            y_copy(m, slot, y_near_down).wait_recv()
            t = sums(m)
            t[...] = t[...] + y_in[slot, 1] + y_in[slot, 2]

    def unit(n, carry):
        slot, j = place(n)

        @pl.when(slot == 0)
        def _():
            pltpu.make_async_copy(x_cols(0), xbuf.at[n], own_sem.at[j]).wait()

        @pl.when(slot == 1)
        def _():
            rcopy(x_cols(0), xbuf.at[n], xs.at[0, j], xr.at[0, j], to_h_up).wait_recv()
            x_right2(j).start()

        @pl.when(slot == 2)
        def _():
            rcopy(x_cols(0), xbuf.at[n], xs.at[1, j], xr.at[1, j], to_h_down).wait_recv()
            x_left2(j).start()

        @pl.when(slot == 3)
        def _():
            x_right2(j).wait_recv()
            x_left2(j).wait_recv()

        hi, lo = split(xbuf[n])
        x_hi[...] = hi
        x_lo[...] = lo

        @pl.when(n >= 4)
        def _():
            core_copy(n - 4).wait_send()

        def rows_of(ft, c2):
            rows = pl.ds(pl.multiple_of(ft * tile, tile), tile)
            a_hi = gt_hi[rows, :]
            acc = mm(a_hi, x_hi[...]) + mm(a_hi, x_lo[...]) + mm(gt_lo[rows, :], x_hi[...])
            left, right = acc[:, :128], acc[:, 128:]
            first = core == 0
            kv[pl.ds(pl.multiple_of(n * feats + ft * tile, tile), tile), :] = jnp.where(first, left, right)
            gbuf[pl.ds(pl.multiple_of((n % 4) * feats + ft * tile, tile), tile), :] = jnp.where(first, right, left)
            return c2

        lax.fori_loop(0, feats // tile, rows_of, 0)
        core_copy(n).start()

        @pl.when(n >= 1)
        def _():
            settle(n - 1)

        for slot_k, (a, b, c) in enumerate(((4, 6, 9), (11, 13, 15), (12, 14, 15))):
            @pl.when(n == a)
            def _():
                z_first(slot_k)

            @pl.when(n == b)
            def _():
                z_middle(slot_k)

            @pl.when(n == c)
            def _():
                z_root(slot_k)

        return carry

    lax.fori_loop(0, 16, unit, 0)
    settle(15)
    z_first(3)
    z_middle(3)
    z_root(3)

    out_copy.wait()
    for j in range(4):
        x_right(j).wait_send()
        x_left(j).wait_send()
        x_right2(j).wait_send()
        x_left2(j).wait_send()
    for p in range(1, 5):
        share(p).wait_send()
    for n in range(12, 16):
        core_copy(n).wait_send()
    for slot in range(4):
        first = (0, 4, 5, 12)[slot]
        by = (1, 2, 2, 1)[slot]
        y_copy(first, slot, y_far_lo).wait_send()
        y_copy(first, slot, y_far_hi).wait_send()
        y_copy(first + by, slot, y_near_up).wait_send()
        y_copy(first + 2 * by, slot, y_near_down).wait_send()
        z_drain(slot)


def body(tokens_x, keys, values, grad_out, level_table, level_bins):
    tokens, heads, hd = keys.shape
    feats = heads * hd
    used = (tokens * lax.axis_size("seq")).bit_length()
    table = jnp.transpose(level_table[:, :, :used], (0, 2, 1))
    quarter = tokens // 4
    dma = pltpu.SemaphoreType.DMA
    stack = max(tokens * heads * 2, 16 * feats)
    hbm = pl.BlockSpec(memory_space=pl.ANY)
    vmem = pl.BlockSpec(memory_space=pltpu.VMEM)
    gq, wq = pl.pallas_call(
        kernel,
        out_shape=(
            jax.ShapeDtypeStruct((tokens * heads, hd), F32),
            jax.ShapeDtypeStruct((128, feats), F32),
        ),
        in_specs=[hbm, hbm, hbm, hbm, vmem, vmem],
        out_specs=(hbm, vmem),
        scratch_shapes=[
            pltpu.VMEM((16, tokens, 256), F32),
            pltpu.VMEM((stack, hd), F32),
            pltpu.VMEM((max(tokens * heads, 4 * feats), hd), F32),
            pltpu.VMEM((tokens * heads, hd), F32),
            pltpu.VMEM((feats, tokens), BF16),
            pltpu.VMEM((feats, tokens), BF16),
            pltpu.VMEM((heads, used, tokens), F32),
            pltpu.VMEM((quarter, quarter), jnp.int32),
            pltpu.VMEM((heads, 4, hd, hd), F32),
            pltpu.VMEM((heads, hd, hd), F32),
            pltpu.VMEM((5, heads, hd, hd), F32),
            pltpu.VMEM((4, feats, 128), F32),
            pltpu.VMEM((4, 3, feats, 128), F32),
            pltpu.VMEM((4, 2, feats, 128), F32),
            pltpu.VMEM((tokens, 256), BF16),
            pltpu.VMEM((tokens, 256), BF16),
            dma((3,)),
            dma,
            dma((4,)),
            dma((4, 4)),
            dma((4, 4)),
            dma((5,)),
            dma((5,)),
            dma((5,)),
            dma((5,)),
            dma((16,)),
            dma((16,)),
            dma((4, 4)),
            dma((4, 4)),
            dma((4, 4)),
            dma((4, 4)),
        ],
        compiler_params=pltpu.CompilerParams(
            collective_id=0, has_side_effects=True, vmem_limit_bytes=63 * 1024 * 1024,
        ),
        name="query_grad",
    )(
        tokens_x,
        keys.reshape(tokens * heads, hd),
        values.reshape(tokens * heads, hd),
        grad_out.reshape(tokens * heads, hd),
        table,
        level_bins.T,
    )
    return gq.reshape(tokens, heads, hd), wq


def solution(mesh):
    in_specs = (
        P("seq", "head"),
        P("seq", "head", None),
        P("seq", "head", None),
        P("seq", "head", None),
        P("head", None, None),
        P("seq", "head"),
    )
    out_specs = (P("seq", "head", None), P("seq", "head"))
    return jax.shard_map(body, mesh=mesh, in_specs=in_specs, out_specs=out_specs, check_vma=False)
```

time: 440 us -> 185 us (0.42); the launches traced: 432 us -> 185 us
  matrix products: 274 us -> 0 us
  Pallas kernels: 0 us -> 177 us
  waiting for transfers between devices: 122 us -> 0 us
  local copies, waits for them, and re-layouts: 21.2 us -> 6.88 us
  between operations: 14.1 us -> 0.65 us
    dot_general x25 -> x0, matrix products: 274 us -> none  [the longest x8 114 us: one_head(): return jnp.dot(scores * mixing, key_piece, precision=HIGH)]
    pallas_call x0 -> x1, Pallas kernels: none -> 177 us  [body(): pl.pallas_call(kernel, out_shape=(jax.ShapeDtypeStruct((tokens * heads, h...]
    reduce_scatter x1 -> x0, waiting for transfers between devices: 110 us -> none  [body(): lax.psum_scatter(jnp.einsum('tc,tf->cf', whole_x, flat, precision=HIGH),...]
    all_gather x2 -> x0, waiting for transfers between devices: 10.8 us -> none  [the longest x1 10.8 us: body(): whole_x = lax.all_gather(tokens_x, 'head', axis=1, tiled=True)]
    unnamed x20 -> x5, local copies, waits for them, and re-layouts: 12.8 us -> 6.88 us
    transpose x1 -> x0, local copies, waits for them, and re-layouts: 5 us -> none  [body(): jnp.transpose(keys, (1, 0, 2))]
  transfers between devices with their start and end apart: 3 -> 0, of which waited for: 2 -> 0; matrix products, arithmetic and copies ran while one was open for 51% -> 0% of each run, Pallas kernels for 0% -> 0%
where the time goes in v1:
time: 185 us
  Pallas kernels  177 us (96%)
  local copies, waits for them, and re-layouts  6.88 us (4%)
    pallas_call x1, Pallas kernels, body(): pl.pallas_call(kernel, out_shape=(jax.ShapeDtypeStruct((tokens * heads, h...  177 us
    unnamed x5, local copies, waits for them, and re-layouts  6.88 us

profile of v1, /device:TPU:64, one launch (start us, length us, event | category | flops | bytes accessed | tf_op | source)
XLA Modules:
  0.0 184.8 jit_solution(13934639207808812831)
XLA Ops:
  0.6 1.6 copy.9
  2.2 177.2 %query_grad.1 = (f32[8192,128]{1,0:T(8,128)}, f32[128,1024]{1,0:T(8,128)}) custom-call(f32[1024,1024]{1,0:T(8,128)} %x_hbm.1, f32[8192,128]{1,0:T(8,128)} %bitcast.8, f32[8192,128]{1,0:T(8,128)} %bitcast.9, f32[8192,128]{1,0:T(8,128)} %bitcast.10, f32[8,16,16]{2,1,0:T(8,128)} %bitcast.11, s32[8,1024]{1,0:T(8,128)} %bitcast.13), custom_call_target="tpu_custom_call" | custom-call | tf_op jit(solution)/shard_map/query_grad/pallas_call | solution.py:514
  179.4 0.0 copy-start
  179.4 4.5 %copy.12 = f32[1024,8,128]{2,1,0:T(8,128)} copy(f32[1024,8,128]{2,1,0:T(8,128)} %bitcast.7) | data formatting | bytes 8388608
  184.0 0.0 copy-done
  184.0 0.8 copy.13
Async XLA Ops:
  179.4 4.5 %copy-start = (f32[128,1024]{1,0:T(8,128)S(1)}, f32[128,1024]{1,0:T(8,128)}, u32[]{:S(2)}) copy-start(f32[128,1024]{1,0:T(8,128)} %get-tuple-element.9) | copy-start | bytes 1572868

commit v2 on v1

--- a/solution.py
+++ b/solution.py
@@ -25,8 +25,8 @@
     x_hbm, k_hbm, v_hbm, g_hbm, tab_ref, bins_ref,
     gq_hbm, wq_ref,
     xbuf, kv, gbuf, oq, gt_hi, gt_lo, wts, lev, chunk_st, state, bucket,
-    core_in, y_in, z_in, x_hi, x_lo,
-    load_sem, out_sem, own_sem, xs, xr, bs, br, ss, sr, cs, cr, ys, yr, zs, zr,
+    core_in, y_in, z_in, z_hop, x_hi, x_lo,
+    load_sem, out_sem, own_sem, xs, xr, bs, br, ss, sr, cs, cr, ys, yr, zs, zr, zh,
 ):
     tokens, width = x_hbm.shape
     heads = tab_ref.shape[0]
@@ -34,7 +34,7 @@
     feats = heads * hd
     quarter = tokens // 4
     half_t = tokens // 2
-    half_f = feats // 2
+    half_f, quart_f = feats // 2, feats // 4
     half_h = heads // 2
     span_bits = tokens.bit_length() - 1
     tile = min(256, feats)
@@ -103,13 +103,18 @@
 
     low_t, high_t = pl.ds(0, half_t), pl.ds(half_t, half_t)
 
-    def x_right2(j):
+    def x_second(j, part, near, rows, kind, dev):
+        cols = pl.ds(0, 256) if part is None else pl.ds(part * 128, 128)
+        sem = j if part is None else 3 + part
         return rcopy(
-            xbuf.at[4 + 2 * j, low_t], xbuf.at[12 + j, low_t], xs.at[2, j], xr.at[2, j], to_h_up)
-
-    def x_left2(j):
-        return rcopy(
-            xbuf.at[5 + 2 * j, high_t], xbuf.at[12 + j, high_t], xs.at[3, j], xr.at[3, j], to_h_down)
+            xbuf.at[near + 2 * j, rows, cols], xbuf.at[12 + j, rows, cols],
+            xs.at[kind, sem], xr.at[kind, sem], dev)
+
+    def x_right2(j, part=None):
+        return x_second(j, part, 4, low_t, 2, to_h_up)
+
+    def x_left2(j, part=None):
+        return x_second(j, part, 5, high_t, 3, to_h_down)
 
     for j in range(4):
         x_right(j).start()
@@ -282,139 +287,162 @@
     out_copy = pltpu.make_async_copy(oq, gq_hbm, out_sem)
     out_copy.start()
 
-    low_f, high_f = pl.ds(0, half_f), pl.ds(half_f, half_f)
-
-    def sums(m, part=None):
-        first, count = (0, feats) if part is None else (part * half_f, half_f)
+    split_at = 15
+
+    def sums(m, first=0, count=feats):
         return kv.at[pl.ds(pl.multiple_of(m * feats + first, 8), count)]
 
-    def core_out(n):
-        return gbuf.at[pl.ds(pl.multiple_of((n % 4) * feats, 8), feats)]
-
-    def core_copy(n):
-        return rcopy(core_out(n), core_in.at[n % 4], cs.at[n], cr.at[n], mate)
-
-    y_far_lo, y_far_hi, y_near_up, y_near_down = 0, 1, 2, 3
-
-    def y_copy(m, slot, kind):
-        if kind == y_far_lo:
-            src, dst, dev = sums(m, 0), y_in.at[slot, 0, low_f], to_y_up
-        elif kind == y_far_hi:
-            src, dst, dev = sums(m, 1), y_in.at[slot, 0, high_f], to_y_down
-        elif kind == y_near_up:
-            src, dst, dev = sums(m), y_in.at[slot, 1], to_y_up
-        else:
-            src, dst, dev = sums(m), y_in.at[slot, 2], to_y_down
-        return rcopy(src, dst, ys.at[slot, kind], yr.at[slot, kind], dev)
-
-    def z_copy(m, slot, kind):
-        if kind == 0:
-            src, dst, dev = sums(m, 0), z_in.at[slot, 0, low_f], to_z_up
-        elif kind == 1:
-            src, dst, dev = sums(m, 1), z_in.at[slot, 1, high_f], to_z_down
-        elif kind == 2:
-            src, dst, dev = sums(m), z_in.at[slot, 1], to_z_down
-        else:
-            src, dst, dev = sums(m), z_in.at[slot, 0], to_z_up
-        return rcopy(src, dst, zs.at[slot, kind], zr.at[slot, kind], dev)
-
-    last_unit = (3, 10, 11, 15)
-    block_of = (h, h_down, h_up, (h + 2) % 4)
-
-    def z_dist(slot):
-        return (z + 4 - block_of[slot]) % 4
-
-    def z_first(slot):
-        m = last_unit[slot]
-
-        @pl.when(z_dist(slot) == 2)
-        def _():
-            z_copy(m, slot, 0).start()
-            z_copy(m, slot, 1).start()
-
-    def z_middle(slot):
-        m = last_unit[slot]
-
-        @pl.when(z_dist(slot) == 1)
-        def _():
-            z_copy(m, slot, 1).wait_recv()
-            s = sums(m, 1)
-            s[...] = s[...] + z_in[slot, 1, half_f:, :]
-            z_copy(m, slot, 2).start()
-
-        @pl.when(z_dist(slot) == 3)
-        def _():
-            z_copy(m, slot, 0).wait_recv()
-            s = sums(m, 0)
-            s[...] = s[...] + z_in[slot, 0, :half_f, :]
-            z_copy(m, slot, 3).start()
-
-    def z_root(slot):
-        m = last_unit[slot]
-
-        @pl.when(z_dist(slot) == 0)
-        def _():
-            z_copy(m, slot, 2).wait_recv()
-            z_copy(m, slot, 3).wait_recv()
-            s = sums(m)
-            wq_ref[...] = (s[...] + z_in[slot, 0] + z_in[slot, 1]).T
-
-    def z_drain(slot):
-        m = last_unit[slot]
-
-        @pl.when(z_dist(slot) == 2)
-        def _():
-            z_copy(m, slot, 0).wait_send()
-            z_copy(m, slot, 1).wait_send()
-
-        @pl.when(z_dist(slot) == 1)
-        def _():
-            z_copy(m, slot, 2).wait_send()
-
-        @pl.when(z_dist(slot) == 3)
-        def _():
-            z_copy(m, slot, 3).wait_send()
-
-    def place(m):
+    def upper(m, first=0, count=half_f):
+        return sums(m, half_f + first, count)
+
+    def core_out(m):
+        return gbuf.at[pl.ds(pl.multiple_of((m % 4) * feats, 8), feats)]
+
+    def core_copy(m):
+        return rcopy(core_out(m), core_in.at[m % 4], cs.at[m], cr.at[m], mate)
+
+    lo, hi = pl.ds(0, quart_f), pl.ds(quart_f, quart_f)
+
+    def y_copy(job, kind, src):
+        dst = (
+            y_in.at[job, 0, lo], y_in.at[job, 0, hi], y_in.at[job, 1, hi],
+            y_in.at[job, 1, lo], y_in.at[job, 2, lo], y_in.at[job, 2, hi],
+        )[kind]
+        dev = (to_y_up, to_y_down, to_y_up, to_y_up, to_y_down, to_y_down)[kind]
+        return rcopy(src, dst, ys.at[job, kind], yr.at[job, kind], dev)
+
+    def y_step(job, rows, m, j):
+        first, second, both = rows(m, 0, quart_f), rows(m, quart_f, quart_f), rows(m, 0, half_f)
+
+        @pl.when(j == 0)
+        def _():
+            y_copy(job, 0, first).start()
+            y_copy(job, 1, second).start()
+
+        @pl.when(j == 1)
+        def _():
+            y_copy(job, 2, second).start()
+            y_copy(job, 0, first).wait_recv()
+            first[...] = first[...] + y_in[job, 0, :quart_f, :]
+            y_copy(job, 3, first).start()
+
+        @pl.when(j == 2)
+        def _():
+            y_copy(job, 4, first).start()
+            y_copy(job, 1, second).wait_recv()
+            second[...] = second[...] + y_in[job, 0, quart_f:, :]
+            y_copy(job, 5, second).start()
+
+        @pl.when(j == 3)
+        def _():
+            for kind in range(2, 6):
+                y_copy(job, kind, first).wait_recv()
+            both[...] = both[...] + y_in[job, 1] + y_in[job, 2]
+
+    def z_far(job, kind, src):
+        dev = (to_z_up, to_z_down)[kind]
+        return rcopy(src, z_hop.at[job], zs.at[job, kind], zh.at[job], dev)
+
+    def z_near(job, place, kind, src):
+        side, part, dev = ((1, lo, to_z_down), (1, hi, to_z_down), (0, hi, to_z_up), (0, lo, to_z_up))[kind]
+        return rcopy(src, z_in.at[place, side, part], zs.at[job, kind % 2], zr.at[place, kind], dev)
+
+    def z_first(job, place, rows, m, dist):
+        first, second = rows(m, 0, quart_f), rows(m, quart_f, quart_f)
+
+        @pl.when(dist == 2)
+        def _():
+            z_far(job, 0, first).start()
+            z_far(job, 1, second).start()
+
+        @pl.when(dist == 1)
+        def _():
+            z_near(job, place, 0, first).start()
+
+        @pl.when(dist == 3)
+        def _():
+            z_near(job, place, 2, second).start()
+
+    def z_middle(job, place, rows, m, dist):
+        first, second = rows(m, 0, quart_f), rows(m, quart_f, quart_f)
+
+        @pl.when(dist == 1)
+        def _():
+            z_far(job, 1, second).wait_recv()
+            second[...] = second[...] + z_hop[job]
+            z_near(job, place, 1, second).start()
+
+        @pl.when(dist == 3)
+        def _():
+            z_far(job, 0, first).wait_recv()
+            first[...] = first[...] + z_hop[job]
+            z_near(job, place, 3, first).start()
+
+    def z_root(job, place, rows, m):
+        both = rows(m, 0, half_f)
+        for kind in range(4):
+            z_near(job, place, kind, rows(m, 0, quart_f)).wait_recv()
+        both[...] = both[...] + z_in[place, 0] + z_in[place, 1]
+
+    def place_of(m):
         near = jnp.logical_and(m >= 4, m < 12)
         slot = jnp.where(m < 4, 0, jnp.where(m < 12, 1 + m % 2, 3))
         j = jnp.where(near, (m - 4) // 2, m % 4)
-        return slot, j
-
-    def settle(m):
-        slot, j = place(m)
+        block = jnp.where(slot == 0, h, jnp.where(slot == 1, h + 3, jnp.where(slot == 2, h + 1, h + 2)))
+        return slot, j, (z + 8 - block) % 4
+
+    def when_mine(step, act):
+        halves = jnp.where(step == split_at, core == 0, core == 1)
+        mine = jnp.logical_and(
+            jnp.logical_and(step >= 0, step <= split_at + 1),
+            jnp.logical_or(step < split_at, halves),
+        )
+
+        @pl.when(mine)
+        def _():
+            m = jnp.where(step > split_at, split_at, step)
+            act(m, *place_of(m))
+
+    def stage_one(m, slot, j, dist):
         core_copy(m).wait_recv()
         s = sums(m)
         s[...] = s[...] + core_in[m % 4]
-
-        @pl.when(j == 0)
-        def _():
-            y_copy(m, slot, y_far_lo).start()
-            y_copy(m, slot, y_far_hi).start()
-
-        @pl.when(j == 1)
-        def _():
-            y_copy(m, slot, y_far_lo).wait_recv()
-            t = sums(m, 0)
-            t[...] = t[...] + y_in[slot, 0, :half_f, :]
-            y_copy(m, slot, y_near_up).start()
-
-        @pl.when(j == 2)
-        def _():
-            y_copy(m, slot, y_far_hi).wait_recv()
-            t = sums(m, 1)
-            t[...] = t[...] + y_in[slot, 0, half_f:, :]
-            y_copy(m, slot, y_near_down).start()
+        z_first(m, j, upper, m, dist)
+        y_step(slot, sums, m, j)
 
         @pl.when(j == 3)
         def _():
-            y_copy(m, slot, y_near_up).wait_recv()
-            y_copy(m, slot, y_near_down).wait_recv()
-            t = sums(m)
-            t[...] = t[...] + y_in[slot, 1] + y_in[slot, 2]
-
-    def unit(n, carry):
-        slot, j = place(n)
+            z_first(16 + slot, 4, sums, m, dist)
+
+    def stage_two(m, slot, j, dist):
+        z_middle(m, j, upper, m, dist)
+
+        @pl.when(j == 3)
+        def _():
+            z_middle(16 + slot, 4, sums, m, dist)
+
+    def stage_three(m, slot, j, dist):
+        @pl.when(dist == 0)
+        def _():
+            z_root(m, j, upper, m)
+            y_step(4, upper, m, j)
+
+            @pl.when(j == 3)
+            def _():
+                z_root(16 + slot, 4, sums, m)
+                wq_ref[...] = sums(m)[...].T
+
+    def times(rows, cols):
+        a_hi = gt_hi[rows, :]
+        return (
+            mm(a_hi, x_hi[:, cols]) + mm(a_hi, x_lo[:, cols]) + mm(gt_lo[rows, :], x_hi[:, cols])
+        )
+
+    def tile_rows(ft, m=0):
+        return pl.ds(pl.multiple_of(m * feats + ft * tile, tile), tile)
+
+    def arrive(n):
+        slot, j, _ = place_of(n)
 
         @pl.when(slot == 0)
         def _():
@@ -423,82 +451,136 @@
         @pl.when(slot == 1)
         def _():
             rcopy(x_cols(0), xbuf.at[n], xs.at[0, j], xr.at[0, j], to_h_up).wait_recv()
-            x_right2(j).start()
+
+            @pl.when(j < 3)
+            def _():
+                x_right2(j).start()
+
+            @pl.when(j == 3)
+            def _():
+                x_right2(3, 0).start()
+                x_right2(3, 1).start()
 
         @pl.when(slot == 2)
         def _():
             rcopy(x_cols(0), xbuf.at[n], xs.at[1, j], xr.at[1, j], to_h_down).wait_recv()
-            x_left2(j).start()
+
+            @pl.when(j < 3)
+            def _():
+                x_left2(j).start()
+
+            @pl.when(j == 3)
+            def _():
+                x_left2(3, 0).start()
+                x_left2(3, 1).start()
 
         @pl.when(slot == 3)
         def _():
             x_right2(j).wait_recv()
             x_left2(j).wait_recv()
 
-        hi, lo = split(xbuf[n])
-        x_hi[...] = hi
-        x_lo[...] = lo
+    def whole_unit(n):
+        arrive(n)
+        high, low = split(xbuf[n])
+        x_hi[...] = high
+        x_lo[...] = low
 
         @pl.when(n >= 4)
         def _():
             core_copy(n - 4).wait_send()
 
         def rows_of(ft, c2):
-            rows = pl.ds(pl.multiple_of(ft * tile, tile), tile)
-            a_hi = gt_hi[rows, :]
-            acc = mm(a_hi, x_hi[...]) + mm(a_hi, x_lo[...]) + mm(gt_lo[rows, :], x_hi[...])
+            acc = times(tile_rows(ft), slice(0, 256))
             left, right = acc[:, :128], acc[:, 128:]
             first = core == 0
-            kv[pl.ds(pl.multiple_of(n * feats + ft * tile, tile), tile), :] = jnp.where(first, left, right)
-            gbuf[pl.ds(pl.multiple_of((n % 4) * feats + ft * tile, tile), tile), :] = jnp.where(first, right, left)
+            kv[tile_rows(ft, n), :] = jnp.where(first, left, right)
+            gbuf[tile_rows(ft, n % 4), :] = jnp.where(first, right, left)
             return c2
 
         lax.fori_loop(0, feats // tile, rows_of, 0)
         core_copy(n).start()
 
-        @pl.when(n >= 1)
-        def _():
-            settle(n - 1)
-
-        for slot_k, (a, b, c) in enumerate(((4, 6, 9), (11, 13, 15), (12, 14, 15))):
-            @pl.when(n == a)
-            def _():
-                z_first(slot_k)
-
-            @pl.when(n == b)
-            def _():
-                z_middle(slot_k)
-
-            @pl.when(n == c)
-            def _():
-                z_root(slot_k)
-
+    def half_unit(n):
+        part = n - split_at
+
+        @pl.when(part == 0)
+        def _():
+            x_right2(3, 0).wait_recv()
+            x_left2(3, 0).wait_recv()
+            core_copy(split_at - 4).wait_send()
+
+        @pl.when(part == 1)
+        def _():
+            x_right2(3, 1).wait_recv()
+            x_left2(3, 1).wait_recv()
+
+        high, low = split(xbuf[split_at, :, pl.ds(pl.multiple_of(part * 128, 128), 128)])
+        x_hi[:, :128] = high
+        x_lo[:, :128] = low
+
+        def kept(ft, c2):
+            kv[tile_rows(ft, split_at), :] = times(tile_rows(ft), slice(0, 128))
+            return c2
+
+        def given(ft, c2):
+            gbuf[tile_rows(ft, split_at % 4), :] = times(tile_rows(ft), slice(0, 128))
+            return c2
+
+        @pl.when(core == part)
+        def _():
+            lax.fori_loop(0, feats // tile, kept, 0)
+
+        @pl.when(core != part)
+        def _():
+            lax.fori_loop(0, feats // tile, given, 0)
+            core_copy(split_at).start()
+
+    def step(n, carry):
+        @pl.when(n < split_at)
+        def _():
+            whole_unit(n)
+
+        @pl.when(jnp.logical_or(n == split_at, n == split_at + 1))
+        def _():
+            half_unit(n)
+
+        when_mine(n - 1, stage_one)
+        when_mine(n - 2, stage_two)
+        when_mine(n - 3, stage_three)
         return carry
 
-    lax.fori_loop(0, 16, unit, 0)
-    settle(15)
-    z_first(3)
-    z_middle(3)
-    z_root(3)
+    lax.fori_loop(0, split_at + 5, step, 0)
 
     out_copy.wait()
     for j in range(4):
         x_right(j).wait_send()
         x_left(j).wait_send()
-        x_right2(j).wait_send()
-        x_left2(j).wait_send()
+    for j, part in ((0, None), (1, None), (2, None), (3, 0), (3, 1)):
+        x_right2(j, part).wait_send()
+        x_left2(j, part).wait_send()
     for p in range(1, 5):
         share(p).wait_send()
-    for n in range(12, 16):
-        core_copy(n).wait_send()
-    for slot in range(4):
-        first = (0, 4, 5, 12)[slot]
-        by = (1, 2, 2, 1)[slot]
-        y_copy(first, slot, y_far_lo).wait_send()
-        y_copy(first, slot, y_far_hi).wait_send()
-        y_copy(first + by, slot, y_near_up).wait_send()
-        y_copy(first + 2 * by, slot, y_near_down).wait_send()
-        z_drain(slot)
+    for m in range(12, 16):
+        core_copy(m).wait_send()
+
+    def y_drain(job, carry):
+        for kind in range(6):
+            y_copy(job, kind, sums(0, 0, quart_f)).wait_send()
+        return carry
+
+    def z_drain(job, carry):
+        m = jnp.where(job < 16, job, jnp.where(job == 16, 0, jnp.where(job == 19, 12, job - 13)))
+        _, _, dist = place_of(m)
+
+        @pl.when(dist != 0)
+        def _():
+            for kind in range(2):
+                z_far(job, kind, sums(0, 0, quart_f)).wait_send()
+
+        return carry
+
+    lax.fori_loop(0, 5, y_drain, 0)
+    lax.fori_loop(0, 20, z_drain, 0)
 
 
 def body(tokens_x, keys, values, grad_out, level_table, level_bins):
@@ -532,25 +614,27 @@
             pltpu.VMEM((heads, hd, hd), F32),
             pltpu.VMEM((5, heads, hd, hd), F32),
             pltpu.VMEM((4, feats, 128), F32),
-            pltpu.VMEM((4, 3, feats, 128), F32),
-            pltpu.VMEM((4, 2, feats, 128), F32),
+            pltpu.VMEM((5, 3, feats // 2, 128), F32),
+            pltpu.VMEM((5, 2, feats // 2, 128), F32),
+            pltpu.VMEM((20, feats // 4, 128), F32),
             pltpu.VMEM((tokens, 256), BF16),
             pltpu.VMEM((tokens, 256), BF16),
             dma((3,)),
             dma,
             dma((4,)),
-            dma((4, 4)),
-            dma((4, 4)),
+            dma((4, 5)),
+            dma((4, 5)),
             dma((5,)),
             dma((5,)),
             dma((5,)),
             dma((5,)),
             dma((16,)),
             dma((16,)),
-            dma((4, 4)),
-            dma((4, 4)),
-            dma((4, 4)),
-            dma((4, 4)),
+            dma((5, 6)),
+            dma((5, 6)),
+            dma((20, 2)),
+            dma((5, 4)),
+            dma((20,)),
         ],
         compiler_params=pltpu.CompilerParams(
             collective_id=0, has_side_effects=True, vmem_limit_bytes=63 * 1024 * 1024,

time: 185 us -> 178 us (0.962); the launches traced: 185 us -> 175 us
  Pallas kernels: 177 us -> 167 us
    pallas_call x1, Pallas kernels: 177 us -> 167 us  [body(): pl.pallas_call(kernel, out_shape=(jax.ShapeDtypeStruct((tokens * heads, h...]
where the time goes in v2:
time: 178 us; the launch traced here: 175 us
  Pallas kernels  167 us (94%)
  local copies, waits for them, and re-layouts  6.88 us (4%)
    pallas_call x1, Pallas kernels, body(): pl.pallas_call(kernel, out_shape=(jax.ShapeDtypeStruct((tokens * heads, h...  167 us
    unnamed x5, local copies, waits for them, and re-layouts  6.88 us

profile of v2, /device:TPU:64, one launch (start us, length us, event | category | flops | bytes accessed | tf_op | source)
XLA Modules:
  0.0 174.5 jit_solution(640171888411718880)
XLA Ops:
  0.6 1.6 copy.9
  2.2 167.0 %query_grad.1 = (f32[8192,128]{1,0:T(8,128)}, f32[128,1024]{1,0:T(8,128)}) custom-call(f32[1024,1024]{1,0:T(8,128)} %x_hbm.1, f32[8192,128]{1,0:T(8,128)} %bitcast.8, f32[8192,128]{1,0:T(8,128)} %bitcast.9, f32[8192,128]{1,0:T(8,128)} %bitcast.10, f32[8,16,16]{2,1,0:T(8,128)} %bitcast.11, s32[8,1024]{1,0:T(8,128)} %bitcast.13), custom_call_target="tpu_custom_call" | custom-call | tf_op jit(solution)/shard_map/query_grad/pallas_call | solution.py:596
  169.2 0.0 copy-start
  169.2 4.5 %copy.12 = f32[1024,8,128]{2,1,0:T(8,128)} copy(f32[1024,8,128]{2,1,0:T(8,128)} %bitcast.7) | data formatting | bytes 8388608
  173.7 0.0 copy-done
  173.7 0.8 copy.13
Async XLA Ops:
  169.2 4.5 %copy-start = (f32[128,1024]{1,0:T(8,128)S(1)}, f32[128,1024]{1,0:T(8,128)}, u32[]{:S(2)}) copy-start(f32[128,1024]{1,0:T(8,128)} %get-tuple-element.9) | copy-start | bytes 1572868

commit v3 on v2

--- a/solution.py
+++ b/solution.py
@@ -93,13 +93,13 @@
         return x_hbm.at[:, pl.ds(pl.multiple_of(yt * 256, 256), 256)]
 
     def x_own(j):
-        return pltpu.make_async_copy(x_cols(j), xbuf.at[j], own_sem.at[j])
+        return pltpu.make_async_copy(x_cols(j), xbuf.at[3 * j], own_sem.at[j])
 
     def x_right(j):
-        return rcopy(x_cols(j), xbuf.at[4 + 2 * j], xs.at[0, j], xr.at[0, j], to_h_up)
+        return rcopy(x_cols(j), xbuf.at[3 * j + 1], xs.at[0, j], xr.at[0, j], to_h_up)
 
     def x_left(j):
-        return rcopy(x_cols(j), xbuf.at[5 + 2 * j], xs.at[1, j], xr.at[1, j], to_h_down)
+        return rcopy(x_cols(j), xbuf.at[3 * j + 2], xs.at[1, j], xr.at[1, j], to_h_down)
 
     low_t, high_t = pl.ds(0, half_t), pl.ds(half_t, half_t)
 
@@ -107,14 +107,14 @@
         cols = pl.ds(0, 256) if part is None else pl.ds(part * 128, 128)
         sem = j if part is None else 3 + part
         return rcopy(
-            xbuf.at[near + 2 * j, rows, cols], xbuf.at[12 + j, rows, cols],
+            xbuf.at[near + 3 * j, rows, cols], xbuf.at[12 + j, rows, cols],
             xs.at[kind, sem], xr.at[kind, sem], dev)
 
     def x_right2(j, part=None):
-        return x_second(j, part, 4, low_t, 2, to_h_up)
+        return x_second(j, part, 1, low_t, 2, to_h_up)
 
     def x_left2(j, part=None):
-        return x_second(j, part, 5, high_t, 3, to_h_down)
+        return x_second(j, part, 2, high_t, 3, to_h_down)
 
     for j in range(4):
         x_right(j).start()
@@ -173,7 +173,7 @@
 
     for hh in range(heads):
         row = bins_ref[hh:hh + 1, :]
-        tab = tab_ref[hh]
+        tab = tab_ref[hh][:, :wts.shape[1]].T
         acc = jnp.zeros((tab.shape[0], tokens), F32)
         for b in range(tab.shape[1]):
             acc = acc + jnp.where(row == b, tab[:, b:b + 1], 0.0)
@@ -221,23 +221,14 @@
             parts.append(out)
         oq[head_rows(hh), :] = jnp.concatenate(parts, axis=0)
 
-        @pl.when(hh == heads // 4 - 1)
-        def _():
-            pump(0)
-
-        @pl.when(hh == heads - 2)
+        @pl.when(hh == heads // 2 - 1)
         def _():
             pump(1)
 
         return carry
 
-    if heads >= 4:
-        lax.fori_loop(0, heads, local_of, 0)
-    else:
-        for hh in range(heads):
-            local_of(hh, 0)
-        pump(0)
-        pump(1)
+    pump(0)
+    lax.fori_loop(0, heads, local_of, 0)
 
     bits = [core, y % 2, y // 2, z % 2, z // 2]
 
@@ -301,6 +292,12 @@
     def core_copy(m):
         return rcopy(core_out(m), core_in.at[m % 4], cs.at[m], cr.at[m], mate)
 
+    def last_core_copy(part):
+        slot, rows = split_at % 4, pl.ds(part * half_f, half_f)
+        return rcopy(
+            gbuf.at[pl.ds(slot * feats + part * half_f, half_f)], core_in.at[slot, rows],
+            cs.at[split_at + part], cr.at[split_at + part], mate)
+
     lo, hi = pl.ds(0, quart_f), pl.ds(quart_f, quart_f)
 
     def y_copy(job, kind, src):
@@ -384,12 +381,13 @@
             z_near(job, place, kind, rows(m, 0, quart_f)).wait_recv()
         both[...] = both[...] + z_in[place, 0] + z_in[place, 1]
 
+    def dist_of(slot):
+        block = jnp.where(slot == 0, h, jnp.where(slot == 1, h + 3, jnp.where(slot == 2, h + 1, h + 2)))
+        return (z + 8 - block) % 4
+
     def place_of(m):
-        near = jnp.logical_and(m >= 4, m < 12)
-        slot = jnp.where(m < 4, 0, jnp.where(m < 12, 1 + m % 2, 3))
-        j = jnp.where(near, (m - 4) // 2, m % 4)
-        block = jnp.where(slot == 0, h, jnp.where(slot == 1, h + 3, jnp.where(slot == 2, h + 1, h + 2)))
-        return slot, j, (z + 8 - block) % 4
+        slot = jnp.where(m < 12, m % 3, 3)
+        return slot, jnp.where(m < 12, m // 3, m - 12), dist_of(slot)
 
     def when_mine(step, act):
         halves = jnp.where(step == split_at, core == 0, core == 1)
@@ -404,22 +402,36 @@
             act(m, *place_of(m))
 
     def stage_one(m, slot, j, dist):
-        core_copy(m).wait_recv()
-        s = sums(m)
-        s[...] = s[...] + core_in[m % 4]
+        @pl.when(m < split_at)
+        def _():
+            core_copy(m).wait_recv()
+
+        @pl.when(m == split_at)
+        def _():
+            last_core_copy(0).wait_recv()
+
+        s = sums(m, 0, half_f)
+        s[...] = s[...] + core_in[m % 4, :half_f, :]
+        y_step(slot, sums, m, j)
+
+        @pl.when(j == 3)
+        def _():
+            z_first(16 + slot, 4, sums, m, dist)
+
+        @pl.when(m == split_at)
+        def _():
+            last_core_copy(1).wait_recv()
+
+        s = upper(m)
+        s[...] = s[...] + core_in[m % 4, half_f:, :]
         z_first(m, j, upper, m, dist)
-        y_step(slot, sums, m, j)
-
+
+    def stage_two(m, slot, j, dist):
         @pl.when(j == 3)
         def _():
-            z_first(16 + slot, 4, sums, m, dist)
-
-    def stage_two(m, slot, j, dist):
+            z_middle(16 + slot, 4, sums, m, dist)
+
         z_middle(m, j, upper, m, dist)
-
-        @pl.when(j == 3)
-        def _():
-            z_middle(16 + slot, 4, sums, m, dist)
 
     def stage_three(m, slot, j, dist):
         @pl.when(dist == 0)
@@ -432,11 +444,9 @@
                 z_root(16 + slot, 4, sums, m)
                 wq_ref[...] = sums(m)[...].T
 
-    def times(rows, cols):
+    def times(rows):
         a_hi = gt_hi[rows, :]
-        return (
-            mm(a_hi, x_hi[:, cols]) + mm(a_hi, x_lo[:, cols]) + mm(gt_lo[rows, :], x_hi[:, cols])
-        )
+        return mm(a_hi, x_hi[...]) + mm(a_hi, x_lo[...]) + mm(gt_lo[rows, :], x_hi[...])
 
     def tile_rows(ft, m=0):
         return pl.ds(pl.multiple_of(m * feats + ft * tile, tile), tile)
@@ -490,7 +500,7 @@
             core_copy(n - 4).wait_send()
 
         def rows_of(ft, c2):
-            acc = times(tile_rows(ft), slice(0, 256))
+            acc = times(tile_rows(ft))
             left, right = acc[:, :128], acc[:, 128:]
             first = core == 0
             kv[tile_rows(ft, n), :] = jnp.where(first, left, right)
@@ -516,40 +526,59 @@
 
         high, low = split(xbuf[split_at, :, pl.ds(pl.multiple_of(part * 128, 128), 128)])
         x_hi[:, :128] = high
-        x_lo[:, :128] = low
+        x_hi[:, 128:] = low
+
+        def narrow(rows):
+            both = mm(gt_hi[rows, :], x_hi[...])
+            return both[:, :128] + both[:, 128:] + mm(gt_lo[rows, :], x_hi[:, :128])
 
         def kept(ft, c2):
-            kv[tile_rows(ft, split_at), :] = times(tile_rows(ft), slice(0, 128))
+            kv[tile_rows(ft, split_at), :] = narrow(tile_rows(ft))
             return c2
 
         def given(ft, c2):
-            gbuf[tile_rows(ft, split_at % 4), :] = times(tile_rows(ft), slice(0, 128))
+            gbuf[tile_rows(ft, split_at % 4), :] = narrow(tile_rows(ft))
+
+            @pl.when(ft == tiles // 2 - 1)
+            def _():
+                last_core_copy(0).start()
+
             return c2
 
+        tiles = feats // tile
+
         @pl.when(core == part)
         def _():
-            lax.fori_loop(0, feats // tile, kept, 0)
+            lax.fori_loop(0, tiles, kept, 0)
 
         @pl.when(core != part)
         def _():
-            lax.fori_loop(0, feats // tile, given, 0)
-            core_copy(split_at).start()
-
-    def step(n, carry):
-        @pl.when(n < split_at)
+            lax.fori_loop(0, tiles, given, 0)
+            last_core_copy(1).start()
+
+    def due(t, lag, late):
+        m = jnp.where(jnp.logical_and(t >= lag, t < 12 + lag), t - lag, -1)
+        for i, when in enumerate(late):
+            m = jnp.where(t == when, 12 + i, m)
+        return m
+
+    def step(t, carry):
+        n = due(t, 0, (17, 20, 23, 26, 28))
+
+        @pl.when(jnp.logical_and(n >= 0, n < split_at))
         def _():
             whole_unit(n)
 
-        @pl.when(jnp.logical_or(n == split_at, n == split_at + 1))
+        @pl.when(n >= split_at)
         def _():
             half_unit(n)
 
-        when_mine(n - 1, stage_one)
-        when_mine(n - 2, stage_two)
-        when_mine(n - 3, stage_three)
+        when_mine(due(t, 1, (18, 21, 24, 27, 29)), stage_one)
+        when_mine(due(t, 3, (19, 22, 25, 28, 30)), stage_two)
+        when_mine(due(t, 5, (20, 23, 26, 30, 31)), stage_three)
         return carry
 
-    lax.fori_loop(0, split_at + 5, step, 0)
+    lax.fori_loop(0, 32, step, 0)
 
     out_copy.wait()
     for j in range(4):
@@ -560,8 +589,10 @@
         x_left2(j, part).wait_send()
     for p in range(1, 5):
         share(p).wait_send()
-    for m in range(12, 16):
+    for m in range(12, 15):
         core_copy(m).wait_send()
+    last_core_copy(0).wait_send()
+    last_core_copy(1).wait_send()
 
     def y_drain(job, carry):
         for kind in range(6):
@@ -569,10 +600,10 @@
         return carry
 
     def z_drain(job, carry):
-        m = jnp.where(job < 16, job, jnp.where(job == 16, 0, jnp.where(job == 19, 12, job - 13)))
-        _, _, dist = place_of(m)
-
-        @pl.when(dist != 0)
+        slot, _, _ = place_of(job)
+        slot = jnp.where(job < 16, slot, job - 16)
+
+        @pl.when(dist_of(slot) != 0)
         def _():
             for kind in range(2):
                 z_far(job, kind, sums(0, 0, quart_f)).wait_send()
@@ -587,7 +618,6 @@
     tokens, heads, hd = keys.shape
     feats = heads * hd
     used = (tokens * lax.axis_size("seq")).bit_length()
-    table = jnp.transpose(level_table[:, :, :used], (0, 2, 1))
     quarter = tokens // 4
     dma = pltpu.SemaphoreType.DMA
     stack = max(tokens * heads * 2, 16 * feats)
@@ -628,8 +658,8 @@
             dma((5,)),
             dma((5,)),
             dma((5,)),
-            dma((16,)),
-            dma((16,)),
+            dma((17,)),
+            dma((17,)),
             dma((5, 6)),
             dma((5, 6)),
             dma((20, 2)),
@@ -645,7 +675,7 @@
         keys.reshape(tokens * heads, hd),
         values.reshape(tokens * heads, hd),
         grad_out.reshape(tokens * heads, hd),
-        table,
+        level_table,
         level_bins.T,
     )
     return gq.reshape(tokens, heads, hd), wq

time: 178 us -> 169 us (0.949)
  Pallas kernels: 167 us -> 160 us
    pallas_call x1, Pallas kernels: 167 us -> 160 us  [body(): pl.pallas_call(kernel, out_shape=(jax.ShapeDtypeStruct((tokens * heads, h...]
    unnamed x5 -> x4, local copies, waits for them, and re-layouts: 6.88 us -> 5.33 us
where the time goes in v3:
time: 169 us; the launch traced here: 166 us
  Pallas kernels  160 us (95%)
  local copies, waits for them, and re-layouts  5.33 us (3%)
    pallas_call x1, Pallas kernels, body(): pl.pallas_call(kernel, out_shape=(jax.ShapeDtypeStruct((tokens * heads, h...  160 us
    unnamed x4, local copies, waits for them, and re-layouts  5.33 us

profile of v3, /device:TPU:64, one launch (start us, length us, event | category | flops | bytes accessed | tf_op | source)
XLA Modules:
  0.0 166.3 jit_solution(3255681402630773416)
XLA Ops:
  0.6 160.3 %query_grad.1 = (f32[8192,128]{1,0:T(8,128)}, f32[128,1024]{1,0:T(8,128)}) custom-call(f32[1024,1024]{1,0:T(8,128)} %x_hbm.1, f32[8192,128]{1,0:T(8,128)} %bitcast.6, f32[8192,128]{1,0:T(8,128)} %bitcast.7, f32[8192,128]{1,0:T(8,128)} %bitcast.8, f32[8,16,17]{2,1,0:T(8,128)} %tab_ref.1, s32[8,1024]{1,0:T(8,128)} %bitcast.9), custom_call_target="tpu_custom_call" | custom-call | tf_op jit(solution)/shard_map/query_grad/pallas_call | solution.py:626
  161.0 0.0 copy-start
  161.0 4.5 %copy.10 = f32[1024,8,128]{2,1,0:T(8,128)} copy(f32[1024,8,128]{2,1,0:T(8,128)} %bitcast.5) | data formatting | bytes 8388608
  165.5 0.0 copy-done
  165.5 0.8 copy.11
Async XLA Ops:
  161.0 4.5 %copy-start = (f32[128,1024]{1,0:T(8,128)S(1)}, f32[128,1024]{1,0:T(8,128)}, u32[]{:S(2)}) copy-start(f32[128,1024]{1,0:T(8,128)} %get-tuple-element.9) | copy-start | bytes 1572868

commit v4 on v3

--- a/solution.py
+++ b/solution.py
@@ -612,6 +612,25 @@
 
     lax.fori_loop(0, 5, y_drain, 0)
     lax.fori_loop(0, 20, z_drain, 0)
+
+
+PIECES = 8
+
+
+def hand_over(gq_in, wq_in, gq_out, wq_out, gq_buf, wq_buf, in_sem, out_sem):
+    count = gq_buf.shape[0] // PIECES
+    parts = [pl.ds(i * count, count) for i in range(PIECES)]
+    fetch = [pltpu.make_async_copy(gq_in.at[p], gq_buf.at[p], in_sem.at[i]) for i, p in enumerate(parts)]
+    store = [pltpu.make_async_copy(gq_buf.at[p], gq_out.at[p], out_sem.at[i]) for i, p in enumerate(parts)]
+    fetch.append(pltpu.make_async_copy(wq_in, wq_buf, in_sem.at[PIECES]))
+    store.append(pltpu.make_async_copy(wq_buf, wq_out, out_sem.at[PIECES]))
+    for c in fetch:
+        c.start()
+    for f, c in zip(fetch, store):
+        f.wait()
+        c.start()
+    for c in store:
+        c.wait()
 
 
 def body(tokens_x, keys, values, grad_out, level_table, level_bins):
@@ -678,6 +697,21 @@
         level_table,
         level_bins.T,
     )
+    rows = tokens * heads
+    gq, wq = pl.pallas_call(
+        hand_over,
+        out_shape=(jax.ShapeDtypeStruct((rows, hd), F32), jax.ShapeDtypeStruct(wq.shape, F32)),
+        in_specs=[hbm, hbm],
+        out_specs=(hbm, hbm),
+        scratch_shapes=[
+            pltpu.VMEM((rows, hd), F32),
+            pltpu.VMEM(wq.shape, F32),
+            dma((PIECES + 1,)),
+            dma((PIECES + 1,)),
+        ],
+        compiler_params=pltpu.CompilerParams(vmem_limit_bytes=62 * 1024 * 1024),
+        name="hand_over",
+    )(gq, wq)
     return gq.reshape(tokens, heads, hd), wq
 
 

time: 169 us -> 167 us (0.988)
  local copies, waits for them, and re-layouts: 5.33 us -> 0 us
  Pallas kernels: 160 us -> 165 us
    unnamed x4 -> x0, local copies, waits for them, and re-layouts: 5.33 us -> none
    pallas_call x0 -> x1, Pallas kernels: none -> 4.16 us  [body(): pl.pallas_call(hand_over, out_shape=(jax.ShapeDtypeStruct((rows, hd), F32...]
where the time goes in v4:
time: 167 us; the launch traced here: 165 us
  Pallas kernels  165 us (99%)
    pallas_call x1, Pallas kernels, body(): pl.pallas_call(kernel, out_shape=(jax.ShapeDtypeStruct((tokens * heads, h...  160 us
    pallas_call x1, Pallas kernels, body(): pl.pallas_call(hand_over, out_shape=(jax.ShapeDtypeStruct((rows, hd), F32...  4.16 us

profile of v4, /device:TPU:64, one launch (start us, length us, event | category | flops | bytes accessed | tf_op | source)
XLA Modules:
  0.0 165.1 jit_solution(5192377813822167646)
XLA Ops:
  0.6 160.3 %query_grad.1 = (f32[8192,128]{1,0:T(8,128)}, f32[128,1024]{1,0:T(8,128)}) custom-call(f32[1024,1024]{1,0:T(8,128)} %x_hbm.1, f32[8192,128]{1,0:T(8,128)} %bitcast.5, f32[8192,128]{1,0:T(8,128)} %bitcast.6, f32[8192,128]{1,0:T(8,128)} %bitcast.7, f32[8,16,17]{2,1,0:T(8,128)} %tab_ref.1, s32[8,1024]{1,0:T(8,128)} %bitcast.8), custom_call_target="tpu_custom_call" | custom-call | tf_op jit(solution)/shard_map/query_grad/pallas_call | solution.py:645
  161.0 4.2 %hand_over.1 = (f32[8192,128]{1,0:T(8,128)}, f32[128,1024]{1,0:T(8,128)}) custom-call(f32[8192,128]{1,0:T(8,128)} %get-tuple-element.6.gq_in, f32[128,1024]{1,0:T(8,128)} %get-tuple-element.7.wq_in), custom_call_target="tpu_custom_call" | custom-call | tf_op jit(solution)/shard_map/hand_over/pallas_call | solution.py:701

commit v5 on v4

--- a/solution.py
+++ b/solution.py
@@ -563,7 +563,7 @@
         return m
 
     def step(t, carry):
-        n = due(t, 0, (17, 20, 23, 26, 28))
+        n = due(t, 0, (17, 20, 23, 26, 29))
 
         @pl.when(jnp.logical_and(n >= 0, n < split_at))
         def _():
@@ -573,12 +573,12 @@
         def _():
             half_unit(n)
 
-        when_mine(due(t, 1, (18, 21, 24, 27, 29)), stage_one)
-        when_mine(due(t, 3, (19, 22, 25, 28, 30)), stage_two)
-        when_mine(due(t, 5, (20, 23, 26, 30, 31)), stage_three)
+        when_mine(due(t, 1, (18, 21, 24, 27, 30)), stage_one)
+        when_mine(due(t, 3, (19, 22, 25, 28, 31)), stage_two)
+        when_mine(due(t, 5, (20, 23, 26, 30, 32)), stage_three)
         return carry
 
-    lax.fori_loop(0, 32, step, 0)
+    lax.fori_loop(0, 33, step, 0)
 
     out_copy.wait()
     for j in range(4):

time: 167 us -> 167 us (level)
  the two profiles are of different devices: /device:TPU:64 before, /device:TPU:65 now
where the time goes in v5:
time: 167 us
  Pallas kernels  167 us (100%)
    pallas_call x1, Pallas kernels, body(): pl.pallas_call(kernel, out_shape=(jax.ShapeDtypeStruct((tokens * heads, h...  162 us
    pallas_call x1, Pallas kernels, body(): pl.pallas_call(hand_over, out_shape=(jax.ShapeDtypeStruct((rows, hd), F32...  4.16 us

profile of v5, /device:TPU:65, one launch (start us, length us, event | category | flops | bytes accessed | tf_op | source)
XLA Modules:
  0.0 167.2 jit_solution(14507601773816327516)
XLA Ops:
  0.6 162.4 %query_grad.1 = (f32[8192,128]{1,0:T(8,128)}, f32[128,1024]{1,0:T(8,128)}) custom-call(f32[1024,1024]{1,0:T(8,128)} %x_hbm.1, f32[8192,128]{1,0:T(8,128)} %bitcast.5, f32[8192,128]{1,0:T(8,128)} %bitcast.6, f32[8192,128]{1,0:T(8,128)} %bitcast.7, f32[8,16,17]{2,1,0:T(8,128)} %tab_ref.1, s32[8,1024]{1,0:T(8,128)} %bitcast.8), custom_call_target="tpu_custom_call" | custom-call | tf_op jit(solution)/shard_map/query_grad/pallas_call | solution.py:645
  163.0 4.2 %hand_over.1 = (f32[8192,128]{1,0:T(8,128)}, f32[128,1024]{1,0:T(8,128)}) custom-call(f32[8192,128]{1,0:T(8,128)} %get-tuple-element.6.gq_in, f32[128,1024]{1,0:T(8,128)} %get-tuple-element.7.wq_in), custom_call_target="tpu_custom_call" | custom-call | tf_op jit(solution)/shard_map/hand_over/pallas_call | solution.py:701
